TPU v7x, 256 devices: a whole 4x4x8 slice. The times are simulated.
256 devices in a mesh: replica: 32 (over z, x_lo, core), tensor: 8 (over x_hi, y).
Axes of the slice: x: 4 (x_hi: 2, x_lo: 2; x = x_hi * 2 + x_lo), y: 4, z: 8, core: 2. Of those that a mesh axis runs over, the one named last changes fastest.
Arguments:
- head_outputs: bfloat16 [16384, 4096], P('replica', 'tensor'), may hold values from -6 to 6
- output_weight: bfloat16 [32, 4096, 4096], P('replica', 'tensor'), may hold values from -0.09375 to 0.09375
- output_grad: bfloat16 [16384, 4096], P(('replica', 'tensor')), may hold values from -6 to 6
- outer_delta: float32 [32, 768, 4096], P('replica', 'tensor'), may hold values from -6 to 6
- local_slice: bfloat16 [32, 768, 4096], P('replica', 'tensor'), may hold values from -6 to 6
- global_slice: float32 [768, 4096], P('tensor', 'replica'), may hold values from -6 to 6
- momentum: float32 [768, 4096], P('tensor', 'replica'), may hold values from -4 to 4
Outputs:
- projected: bfloat16 [16384, 4096], P(('replica', 'tensor'))
- head_grads: bfloat16 [16384, 4096], P('replica', 'tensor')
- weight_grad: bfloat16 [32, 4096, 4096], P('replica', 'tensor')
- merged_slice: bfloat16 [32, 768, 4096], P('replica', 'tensor')
- new_global: float32 [768, 4096], P('tensor', 'replica')
- new_momentum: float32 [768, 4096], P('tensor', 'replica')
All inputs are finite; a program needn't handle non-finite values.
Results may differ from a plain program's by a relative error of at most 0.017.
Values may be sent and summed in bfloat16 or wider, within the bound.
No kernel may reach another device: no remote copies, remote signals or barrier semaphores. Data moves between devices by JAX's collectives and lax.ppermute only.
A program may use at most 64 MiB of HBM per device.

v0:
```python
import jax
import jax.numpy as jnp
from jax import lax
from jax.sharding import PartitionSpec as P


def layer_work(head_outputs, weight, output_grad):
    block = head_outputs
    projected = lax.psum_scatter(
        jnp.dot(block, weight, preferred_element_type=jnp.float32).astype(jnp.bfloat16),
        "tensor",
        scatter_dimension=0,
        tiled=True,
    )
    shard_rows = lax.all_gather(output_grad, "tensor", axis=0, tiled=True)
    product = lax.dot_general(
        shard_rows, weight, (((1,), (1,)), ((), ())), preferred_element_type=jnp.float32
    )
    grad_heads = product
    block = head_outputs
    grad_weight = lax.dot_general(
        block, shard_rows, (((0,), (0,)), ((), ())), preferred_element_type=jnp.float32
    )
    grad_heads, grad_weight = (grad_heads, grad_weight)
    return (projected, grad_heads.astype(jnp.bfloat16), grad_weight.astype(jnp.bfloat16)[None])


def outer_work(outer_delta, local_slice, global_slice, momentum):
    replicas = lax.axis_size("replica")
    delta_part = lax.psum_scatter(
        outer_delta.astype(jnp.bfloat16), "replica", scatter_dimension=2, tiled=True
    ).astype(jnp.float32)[0]
    mean_delta = delta_part / replicas
    new_momentum = 0.9 * momentum + mean_delta
    new_global = global_slice - 0.7 * (mean_delta + 0.9 * new_momentum)
    full_global = lax.all_gather(
        new_global.astype(jnp.bfloat16), "replica", axis=1, tiled=True
    ).astype(new_global.dtype)
    merged_slice = (0.5 * local_slice[0].astype(jnp.float32) + 0.5 * full_global).astype(
        jnp.bfloat16
    )[None]
    return (merged_slice, new_global, new_momentum)


def on_device(
    head_outputs, output_weight, output_grad, outer_delta, local_slice, global_slice, momentum
):
    weight = output_weight[0]
    projected, head_grads, weight_grad = layer_work(head_outputs, weight, output_grad)
    merged_slice, new_global, new_momentum = outer_work(
        outer_delta, local_slice, global_slice, momentum
    )
    return (projected, head_grads, weight_grad, merged_slice, new_global, new_momentum)


def solution(mesh):
    in_specs = (
        P("replica", "tensor"),
        P("replica", "tensor", None),
        P(("replica", "tensor"), None),
        P("replica", "tensor", None),
        P("replica", "tensor", None),
        P("tensor", "replica"),
        P("tensor", "replica"),
    )
    out_specs = (
        P(("replica", "tensor"), None),
        P("replica", "tensor"),
        P("replica", "tensor", None),
        P("replica", "tensor", None),
        P("tensor", "replica"),
        P("tensor", "replica"),
    )
    return jax.shard_map(
        on_device, mesh=mesh, in_specs=in_specs, out_specs=out_specs, check_vma=False
    )
```

profile of v0, /device:TPU:1, one launch (start us, length us, event | category | flops | bytes accessed | tf_op | source)
XLA Modules:
  0.0 250.5 jit_solution(10978857473640024837)
XLA Ops:
  8.0 0.0 copy-start
  8.0 0.0 reduce-scatter.7.cloned.1.call-start
  8.1 1.5 convert_element_type.35
  9.6 2.8 %copy.13 = bf16[1,96,4096]{1,0,2:T(2,128)(2,1)S(1)} copy(bf16[1,96,4096]{2,1,0:T(8,128)(2,1)S(1)} %convert_element_type.35) | data formatting | bytes 1572864
  12.4 1.1 copy.17
  13.5 0.0 reduce-scatter.7.cloned.1.call-update
  13.5 0.0 all-gather.2.cloned.1.call-start
  13.6 0.5 all-gather.2.cloned.1.call-update
  14.1 0.0 reduce-scatter.5.cloned.1.call-start
  14.2 0.0 copy-done
  14.2 6.5 %convolution_convert_fusion.1 = bf16[512,4096]{1,0:T(8,128)(2,1)} fusion(bf16[512,512]{1,0:T(8,128)(2,1)S(1)} %copy-done, bf16[1,512,4096]{2,1,0:T(8,128)(2,1)} %param.8), kind=kOutput, calls=%fused_computation.1 | convolution fusion | flops 2149580800 | bytes 8912896 | tf_op jit(solution)/shard_map/dot_general | solution.py:10
  20.7 0.0 copy-start.3
  20.7 0.0 copy-start.4
  20.7 0.0 copy-start.2
  20.7 0.0 reduce-scatter.5.cloned.1.call-update
  20.7 126.1 %reduce-scatter.7.cloned.1.call-done = bf16[128,96]{1,0:T(8,128)(2,1)} async-done(((bf16[4096,96]{1,0:T(8,128)(2,1)}), bf16[128,96]{1,0:T(8,128)(2,1)}) %reduce-scatter.7.cloned.1.call-update) | async-done | bytes 24592
  146.8 0.8 reshape_bitcast_fusion
  147.6 0.1 copy.14
  147.7 0.0 copy-done.3
  147.7 0.0 copy-done.4
  147.7 0.7 fusion.12
  148.4 36.0 %all_gather.7 = bf16[96,4096]{1,0:T(8,128)(2,1)S(1)} all-gather(bf16[96,128]{1,0:T(8,128)(2,1)S(1)} %get-tuple-element.6), channel_id=1, replica_groups=mesh['replica'=32,'tensor'=8] {'replica'}, dimensions={1}, use_global_device_ids=true | all-gather | bytes 811008 | tf_op jit(solution)/shard_map/all_gather | solution.py:36
  184.4 0.0 copy-done.2
  184.4 1.1 fusion.9
  185.5 0.0 all-gather.2.cloned.1.call-done
  185.5 0.0 copy-start.1
  185.5 0.0 copy-start.5
  185.5 6.7 %fusion = bf16[1,512,4096]{2,1,0:T(8,128)(2,1)} fusion(bf16[512,512]{1,0:T(8,128)(2,1)S(1)} %copy-done, bf16[512,4096]{1,0:T(8,128)(2,1)} %all-gather.2.cloned.1.call-done), kind=kOutput, calls=%fused_computation.2 | convolution fusion | flops 2149580800 | bytes 8912896 | tf_op jit(solution)/shard_map/dot_general | solution.py:21
  192.3 0.0 copy-done.1
  192.3 0.0 copy-done.5
  192.3 3.2 %fusion.6 = bf16[512,512]{1,0:T(8,128)(2,1)} fusion(bf16[512,4096]{1,0:T(8,128)(2,1)S(1)} %copy-done.1, bf16[1,512,4096]{2,1,0:T(8,128)(2,1)S(1)} %copy-done.5), kind=kOutput, calls=%fused_computation.9 | convolution fusion | flops 2147745792 | bytes 8912896 | tf_op jit(solution)/shard_map/dot_general | solution.py:16
  195.4 47.6 %reduce-scatter.5.cloned.1.call-done = bf16[64,4096]{1,0:T(8,128)(2,1)} async-done(((bf16[512,4096]{1,0:T(8,128)(2,1)}), bf16[64,4096]{1,0:T(8,128)(2,1)}) %reduce-scatter.5.cloned.1.call-update) | async-done | bytes 524304 | tf_op jit(solution)/shard_map/reduce_scatter | solution.py:9
Async XLA Ops:
  8.0 6.2 %copy-start = (bf16[512,512]{1,0:T(8,128)(2,1)S(1)}, bf16[512,512]{1,0:T(8,128)(2,1)}, u32[]{:S(2)}) copy-start(bf16[512,512]{1,0:T(8,128)(2,1)} %param.7) | copy-start | bytes 1572868
  8.0 138.8 %reduce-scatter.7.cloned.1.call-start = ((), (), s32[]{:S(2)}) async-start(), calls=%async_computation.4 | async-start | bytes 1081344
  13.5 172.0 %all-gather.2.cloned.1.call-start = ((), (), s32[]{:S(2)}) async-start(), calls=%async_computation.3 | async-start | bytes 4718592 | tf_op jit(solution)/shard_map/all_gather | solution.py:15
  14.1 228.9 %reduce-scatter.5.cloned.1.call-start = ((), (), s32[]{:S(2)}) async-start(), calls=%async_computation.2 | async-start | bytes 4718592 | tf_op jit(solution)/shard_map/reduce_scatter | solution.py:9
  20.7 127.0 %copy-start.3 = (f32[96,128]{1,0:T(8,128)S(1)}, f32[96,128]{1,0:T(8,128)}, u32[]{:S(2)}) copy-start(f32[96,128]{1,0:T(8,128)} %param.12) | copy-start | bytes 147460
  20.7 127.0 %copy-start.4 = (f32[96,128]{1,0:T(8,128)S(1)}, f32[96,128]{1,0:T(8,128)}, u32[]{:S(2)}) copy-start(f32[96,128]{1,0:T(8,128)} %param.13) | copy-start | bytes 147460
  20.7 163.7 %copy-start.2 = (bf16[1,96,4096]{2,1,0:T(8,128)(2,1)S(1)}, bf16[1,96,4096]{2,1,0:T(8,128)(2,1)}, u32[]{:S(2)}) copy-start(bf16[1,96,4096]{2,1,0:T(8,128)(2,1)} %param.11) | copy-start | bytes 2359300
  185.5 6.8 %copy-start.1 = (bf16[512,4096]{1,0:T(8,128)(2,1)S(1)}, bf16[512,4096]{1,0:T(8,128)(2,1)}, u32[]{:S(2)}) copy-start(bf16[512,4096]{1,0:T(8,128)(2,1)} %all-gather.2.cloned.1.call-done) | copy-start | bytes 12582916
  185.5 6.8 %copy-start.5 = (bf16[1,512,4096]{2,1,0:T(8,128)(2,1)S(1)}, bf16[1,512,4096]{2,1,0:T(8,128)(2,1)}, u32[]{:S(2)}) copy-start(bf16[1,512,4096]{2,1,0:T(8,128)(2,1)} %param.8) | copy-start | bytes 12582916
Sparse Core Ops, SparseCore 0:
  13.7 133.0 reduce-scatter.6
  152.0 90.9 reduce-scatter.4
Sparse Core Ops, SparseCore 1:
  16.7 80.0 all-gather.1
where the time goes:
time: 251 us
  waiting for transfers between devices  174 us (69%)
  blocking collectives  36 us (14%)
  matrix products  16.4 us (7%)
  between operations  15.5 us (6%)
  local copies, waits for them, and re-layouts  4.83 us (2%)
  other arithmetic  3.31 us (1%)
    unnamed x4, waiting for transfers between devices  127 us
    reduce_scatter x1, waiting for transfers between devices, layer_work(): lax.psum_scatter(jnp.dot(block, weight, preferred_element_type=jnp.float3...  47.6 us
    all_gather x1, blocking collectives, outer_work(): lax.all_gather(new_global.astype(jnp.bfloat16), 'replica', axis=1, tiled=...  36 us
    dot_general x1, matrix products, layer_work(): lax.dot_general(block, shard_rows, (((0,), (0,)), ((), ())), preferred_el...  6.75 us
    dot_general x1, matrix products, layer_work(): jnp.dot(block, weight, preferred_element_type=jnp.float32)  6.51 us
  transfers between devices with their start and end apart: 3, of which 2 were waited for; matrix products, arithmetic and copies ran while one was open for 8% of the time, Pallas kernels for 0%

commit v1 on v0

v1 whole, which is shorter than its diff:
```python
import functools

import jax
import jax.numpy as jnp
from jax import lax
from jax.experimental import pallas as pl
from jax.experimental.pallas import tpu as pltpu
from jax.sharding import PartitionSpec as P

BF = jnp.bfloat16
F32 = jnp.float32
NY, NX = 4, 2
CX = 2560
CB = 512
LANE = 128
ORDER = (0, 3, 1, 2)
VMEM_LIMIT = 48 * 1024 * 1024


def call(kernel, outs, *args, **kw):
    params = pltpu.CompilerParams(vmem_limit_bytes=VMEM_LIMIT)
    cost = kw.pop("cost", None)
    if cost is None:
        size = sum(a.size * a.dtype.itemsize for a in args) + sum(
            o.size * o.dtype.itemsize for o in jax.tree.leaves(outs)
        )
        cost = pl.CostEstimate(flops=0, bytes_accessed=size, transcendentals=0)
    return pl.pallas_call(
        kernel, out_shape=outs, compiler_params=params, cost_estimate=cost, **kw
    )(*args)


def sds(*shape, dtype=BF):
    return jax.ShapeDtypeStruct(shape, dtype)


def send_y(x, step):
    pairs = [(k * NY + y, k * NY + (y + step) % NY) for k in range(NX) for y in range(NY)]
    return lax.ppermute(x, "tensor", pairs)


def send_x(x):
    pairs = [(k * NY + y, (1 - k) * NY + y) for k in range(NX) for y in range(NY)]
    return lax.ppermute(x, "tensor", pairs)


def send_replica(x, bit):
    return lax.ppermute(x, "replica", [(r, r ^ bit) for r in range(lax.axis_size("replica"))])


def row_block(yi, xi):
    me = lax.axis_index("tensor")
    k, y = me // NY, me % NY
    return ((k + xi) % NX) * NY + (y + ORDER[yi]) % NY


def arrange_rows(a_ref, rel_ref):
    for yi in range(NY):
        for xi in range(NX):
            at = pl.multiple_of(row_block(yi, xi) * 64, 64)
            rel_ref[pl.ds((yi * NX + xi) * 64, 64), :] = a_ref[pl.ds(at, 64), :]


def proj_kernel(a_ref, w_ref, p00, p01, pm, pp, p2a, p2b, py0, py1, rel):
    j = pl.program_id(0)

    @pl.when(j == 0)
    def _():
        arrange_rows(a_ref, rel)

    p = jnp.dot(rel[...], w_ref[...], preferred_element_type=F32).astype(BF)

    @pl.when(j < CX // CB)
    def _():
        p00[...] = p[0:64]
        p01[...] = p[64:128]
        pm[...] = p[128:256]
        pp[...] = p[256:384]
        p2a[...] = p[384:448]
        p2b[...] = p[448:512]

    @pl.when(j >= CX // CB)
    def _():
        for yi in range(NY):
            py0[pl.ds(yi * 64, 64), :] = p[yi * 128 : yi * 128 + 64]
            py1[pl.ds(yi * 64, 64), :] = p[yi * 128 + 64 : yi * 128 + 128]


def in_x(rows):
    return pl.BlockSpec((rows, CB), lambda j: (0, jnp.minimum(j, CX // CB - 1)))


def in_y(rows):
    return pl.BlockSpec((rows, CB), lambda j: (0, jnp.maximum(j - CX // CB, 0)))


def project(a, w):
    d = w.shape[1]
    cy = d - CX
    return call(
        proj_kernel,
        [sds(64, CX), sds(64, CX), sds(128, CX), sds(128, CX), sds(64, CX), sds(64, CX),
         sds(256, cy), sds(256, cy)],
        a, w,
        grid=(d // CB,),
        in_specs=[pl.BlockSpec((512, 512), lambda j: (0, 0)), pl.BlockSpec((512, CB), lambda j: (0, j))],
        out_specs=[in_x(64), in_x(64), in_x(128), in_x(128), in_x(64), in_x(64), in_y(256), in_y(256)],
        scratch_shapes=[pltpu.VMEM((512, 512), BF)],
        cost=pl.CostEstimate(flops=2 * 512 * 512 * d, bytes_accessed=9 << 20, transcendentals=0),
    )


def grads_kernel(a_ref, w_ref, x2, xm, xp, f1, f2, y4, yx, wg, hg, rel, relt, g, acc):
    j = pl.program_id(0)

    @pl.when(j == 0)
    def _():
        arrange_rows(a_ref, rel)
        relt[...] = rel[...].T
        acc[...] = jnp.zeros_like(acc)

    @pl.when(j < CX // CB)
    def _():
        g[0:128, :] = x2[...]
        g[128:256, :] = xm[...]
        g[256:384, :] = xp[...]
        g[384:448, :] = f1[...]
        g[448:512, :] = f2[...]

    @pl.when(j >= CX // CB)
    def _():
        for yi in range(NY):
            g[yi * 128 : yi * 128 + 64, :] = y4[yi * 64 : yi * 64 + 64, :]
            g[yi * 128 + 64 : yi * 128 + 128, :] = yx[yi * 64 : yi * 64 + 64, :]

    wg[...] = jnp.dot(relt[...], g[...], preferred_element_type=F32).astype(BF)
    acc[...] += lax.dot_general(
        g[...], w_ref[...], (((1,), (1,)), ((), ())), preferred_element_type=F32
    )

    @pl.when(j == pl.num_programs(0) - 1)
    def _():
        for yi in range(NY):
            for xi in range(NX):
                at = pl.multiple_of(row_block(yi, xi) * 64, 64)
                hg[pl.ds(at, 64), :] = acc[pl.ds((yi * NX + xi) * 64, 64), :].astype(BF)


def grads(a, w, x2, xm, xp, f1, f2, y4, yx):
    d = w.shape[1]
    full = pl.BlockSpec((512, 512), lambda j: (0, 0))
    col = pl.BlockSpec((512, CB), lambda j: (0, j))
    return call(
        grads_kernel,
        [sds(512, d), sds(512, 512)],
        a, w, x2, xm, xp, f1, f2, y4, yx,
        grid=(d // CB,),
        in_specs=[full, col, in_x(128), in_x(128), in_x(128), in_x(64), in_x(64), in_y(256), in_y(256)],
        out_specs=[col, full],
        scratch_shapes=[
            pltpu.VMEM((512, 512), BF),
            pltpu.VMEM((512, 512), BF),
            pltpu.VMEM((512, CB), BF),
            pltpu.VMEM((512, 512), F32),
        ],
        cost=pl.CostEstimate(flops=4 * 512 * 512 * d, bytes_accessed=14 << 20, transcendentals=0),
    )


def gather_grad(g):
    gx, gy = g[:, :CX], g[:, CX:]
    x1 = send_x(gx)
    ym = send_y(gy, 1)
    yp = send_y(gy, -1)
    x2 = jnp.concatenate([gx, x1], 0)
    xm = send_y(x2, 1)
    xp = send_y(x2, -1)
    y2 = send_y(ym, 1)
    f1 = send_y(xm[:64], 1)
    f2 = send_y(xp[64:], -1)
    y4 = jnp.concatenate([gy, ym, yp, y2], 0)
    yx = send_x(y4)
    return x2, xm, xp, f1, f2, y4, yx


def f32(x):
    return x[...].astype(F32)


def add_low(p_ref, r_ref, o_ref):
    o_ref[0:64, :] = (f32(p_ref.at[0:64, :]) + f32(r_ref)).astype(BF)
    o_ref[64:128, :] = p_ref[64:128, :]


def add_high(p_ref, r_ref, o_ref):
    o_ref[0:64, :] = p_ref[0:64, :]
    o_ref[64:128, :] = (f32(p_ref.at[64:128, :]) + f32(r_ref)).astype(BF)


def cross_kernel(p01, sp, sm, q1):
    q1[...] = (f32(p01) + f32(sp.at[64:128, :]) + f32(sm.at[64:128, :])).astype(BF)


def split_y_kernel(py0, yx, q0, qm, qp, q2):
    for yi, out in enumerate((q0, qm, qp, q2)):
        rows = slice(yi * 64, yi * 64 + 64)
        out[...] = (f32(py0.at[rows, :]) + f32(yx.at[rows, :])).astype(out.dtype)


def add_kernel(a, b, o):
    o[...] = (f32(a) + f32(b)).astype(o.dtype)


def finish_kernel(p00, sp, sm, x, q0, s1, s2, o):
    o[:, 0:CX] = (
        f32(p00) + f32(sp.at[0:64, :]) + f32(sm.at[0:64, :]) + f32(x)
    ).astype(BF)
    o[:, CX:] = (f32(q0) + f32(s1) + f32(s2)).astype(BF)


def scatter_projected(pieces, d):
    p00, p01, pm, pp, p2a, p2b, py0, py1 = pieces
    cy = d - CX
    yx = send_x(py1)
    r1 = send_y(p2a, 1)
    r2 = send_y(p2b, -1)
    pp = call(add_low, sds(128, CX), pp, r1)
    pm = call(add_high, sds(128, CX), pm, r2)
    sp = send_y(pp, 1)
    sm = send_y(pm, -1)
    q0, qm, qp, q2 = call(
        split_y_kernel,
        [sds(64, cy, dtype=F32), sds(64, cy, dtype=F32), sds(64, cy), sds(64, cy)],
        py0, yx,
    )
    w = send_y(q2, -1)
    s1 = send_y(qp, 1)
    qm = call(add_kernel, sds(64, cy), qm, w)
    s2 = send_y(qm, -1)
    x = send_x(call(cross_kernel, sds(64, CX), p01, sp, sm))
    return call(finish_kernel, sds(64, d), p00, sp, sm, x, q0, s1, s2)


def bits():
    r = lax.axis_index("replica")
    return r // 4, (r // 2) % 2, r % 2


def lanes(block):
    start = block * LANE
    return pl.ds(start if isinstance(start, int) else pl.multiple_of(start, LANE), LANE)


def core_send_kernel(d_ref, send):
    _, _, c = bits()
    for i in range(send.shape[1] // LANE):
        send[:, lanes(i)] = d_ref[:, lanes(2 * i + 1 - c)].astype(BF)


def core_add_kernel(d_ref, recv, keep, send):
    _, x, c = bits()
    for i in range(keep.shape[1] // LANE):
        for out, k in ((send, 2 * i + 1 - x), (keep, 2 * i + x)):
            mine = d_ref[:, lanes(2 * k + c)].astype(BF).astype(F32)
            out[:, lanes(i)] = (mine + f32(recv.at[:, lanes(k)])).astype(out.dtype)


def x_add_kernel(keep, recv, glob, mom, total, send):
    n = keep.shape[1]
    t = f32(keep) + f32(recv)
    total[...] = t
    send[:, 0:n] = t.astype(BF)
    send[:, n:] = (glob[...] - 0.567 * mom[...]).astype(BF)


def z_add_kernel(level, keep, mine, recv, total, send):
    n = keep.shape[1]
    z, _, _ = bits()
    bit = (z // level) % 2
    t = f32(keep) + f32(recv.at[:, 0:n])
    total[...] = t
    send[:, 0:n] = t.astype(BF)
    for i in range(level):
        send[:, lanes(n // LANE + bit * level + i)] = mine[:, lanes(n // LANE + i)]
        send[:, lanes(n // LANE + (1 - bit) * level + i)] = recv[:, lanes(n // LANE + i)]


def update_kernel(replicas, level, keep, mine, recv, glob, mom, quarter, new_glob, new_mom):
    n = keep.shape[1]
    z, _, _ = bits()
    bit = (z // level) % 2
    for src, half in ((mine, bit), (recv, 1 - bit)):
        for i in range(level):
            at = lanes(half * level + i)
            mean = (keep[:, at] + f32(recv.at[:, at])) / replicas
            h = f32(src.at[:, lanes(n // LANE + i)])
            quarter[:, at] = (h - 1.33 * mean).astype(BF)
    at = lanes(z)
    mean = (keep[:, at] + f32(recv.at[:, at])) / replicas
    momentum = 0.9 * mom[...] + mean
    new_mom[...] = momentum
    new_glob[...] = glob[...] - 0.7 * (mean + 0.9 * momentum)


def merge_kernel(local, q00, q01, q10, q11, o):
    _, x, c = bits()
    for dx, dc, q in ((0, 0, q00), (0, 1, q01), (1, 0, q10), (1, 1, q11)):
        for i in range(q.shape[1] // LANE):
            xx = x + dx - 2 * x * dx
            cc = c + dc - 2 * c * dc
            at = lanes(4 * i + 2 * xx + cc)
            o[:, at] = (0.5 * f32(local.at[:, at]) + 0.5 * f32(q.at[:, lanes(i)])).astype(BF)


def outer_work(delta, local, glob, mom):
    replicas = lax.axis_size("replica")
    rows, d = delta.shape
    n = d // 4
    recv = send_replica(call(core_send_kernel, sds(rows, d // 2), delta), 1)
    keep, send = call(core_add_kernel, [sds(rows, n, dtype=F32), sds(rows, n)], delta, recv)
    recv = send_replica(send, 2)
    keep, mine = call(
        x_add_kernel, [sds(rows, n, dtype=F32), sds(rows, n + LANE)], keep, recv, glob, mom
    )
    for level in (1, 2):
        recv = send_replica(mine, 4 * level)
        keep, mine = call(
            functools.partial(z_add_kernel, level),
            [sds(rows, n, dtype=F32), sds(rows, n + 2 * level * LANE)],
            keep, mine, recv,
        )
    recv = send_replica(mine, 16)
    small = sds(*glob.shape, dtype=F32)
    q00, new_glob, new_mom = call(
        functools.partial(update_kernel, replicas, 4),
        [sds(rows, n), small, small],
        keep, mine, recv, glob, mom,
    )
    q01 = send_replica(q00, 1)
    q10 = send_replica(q00, 2)
    q11 = send_replica(q10, 1)
    merged = call(merge_kernel, sds(rows, d), local, q00, q01, q10, q11)
    return merged, new_glob, new_mom


def on_device(
    head_outputs, output_weight, output_grad, outer_delta, local_slice, global_slice, momentum
):
    weight = output_weight[0]
    gathered = gather_grad(output_grad)
    pieces = project(head_outputs, weight)
    projected = scatter_projected(pieces, weight.shape[1])
    merged, new_global, new_momentum = outer_work(
        outer_delta[0], local_slice[0], global_slice, momentum
    )
    weight_grad, head_grads = grads(head_outputs, weight, *gathered)
    return (projected, head_grads, weight_grad[None], merged[None], new_global, new_momentum)


def solution(mesh):
    in_specs = (
        P("replica", "tensor"),
        P("replica", "tensor", None),
        P(("replica", "tensor"), None),
        P("replica", "tensor", None),
        P("replica", "tensor", None),
        P("tensor", "replica"),
        P("tensor", "replica"),
    )
    out_specs = (
        P(("replica", "tensor"), None),
        P("replica", "tensor"),
        P("replica", "tensor", None),
        P("replica", "tensor", None),
        P("tensor", "replica"),
        P("tensor", "replica"),
    )
    return jax.shard_map(
        on_device, mesh=mesh, in_specs=in_specs, out_specs=out_specs, check_vma=False
    )
```

time: 251 us -> 122 us (0.49)
  waiting for transfers between devices: 174 us -> 45.7 us
  starting transfers between devices: 0.12 us -> 51.3 us
  blocking collectives: 36 us -> 0 us
  Pallas kernels: 0 us -> 21.5 us
  matrix products: 16.4 us -> 0 us
  between operations: 15.5 us -> 0.89 us
  other arithmetic: 3.31 us -> 0.09 us
  local copies, waits for them, and re-layouts: 4.83 us -> 1.62 us
    unnamed x4 -> x0, waiting for transfers between devices: 127 us -> none
    ppermute x0 -> x26, starting transfers between devices: none -> 51.3 us  [the longest x8 30.4 us: send_replica(): lax.ppermute(x, 'replica', [(r, r ^ bit) for r in range(lax.axis_size('re...]
    reduce_scatter x1 -> x0, waiting for transfers between devices: 47.6 us -> none  [layer_work(): lax.psum_scatter(jnp.dot(block, weight, preferred_element_type=jnp.float3...]
    ppermute x0 -> x26, waiting for transfers between devices: none -> 45.7 us  [the longest x8 35.2 us: send_replica(): lax.ppermute(x, 'replica', [(r, r ^ bit) for r in range(lax.axis_size('re...]
    all_gather x1 -> x0, blocking collectives: 36 us -> none  [outer_work(): lax.all_gather(new_global.astype(jnp.bfloat16), 'replica', axis=1, tiled=...]
    pallas_call x0 -> x15, Pallas kernels: none -> 21.5 us  [call(): pl.pallas_call(kernel, out_shape=outs, compiler_params=params, cost_estim...]
    dot_general x3 -> x0, matrix products: 16.4 us -> none  [the longest x1 6.75 us: layer_work(): lax.dot_general(block, shard_rows, (((0,), (0,)), ((), ())), preferred_el...]
    unnamed x16 -> x14, local copies, waits for them, and re-layouts: 4.83 us -> 1.53 us
  transfers between devices with their start and end apart: 3 -> 26, of which waited for: 2 -> 5; matrix products, arithmetic and copies ran while one was open for 8% -> 0% of each run, Pallas kernels for 0% -> 17%
where the time goes in v1:
time: 122 us; the launch traced here: 121 us
  starting transfers between devices  51.3 us (42%)
  waiting for transfers between devices  45.7 us (37%)
  Pallas kernels  21.5 us (18%)
  local copies, waits for them, and re-layouts  1.62 us (1%)
    ppermute x8, waiting for transfers between devices, send_replica(): lax.ppermute(x, 'replica', [(r, r ^ bit) for r in range(lax.axis_size('re...  35.2 us
    ppermute x8, starting transfers between devices, send_replica(): lax.ppermute(x, 'replica', [(r, r ^ bit) for r in range(lax.axis_size('re...  30.4 us
    pallas_call x15, Pallas kernels, call(): pl.pallas_call(kernel, out_shape=outs, compiler_params=params, cost_estim...  21.5 us
    ppermute x14, starting transfers between devices, send_y(): return lax.ppermute(x, 'tensor', pairs)  13.1 us
    ppermute x14, waiting for transfers between devices, send_y(): return lax.ppermute(x, 'tensor', pairs)  10.5 us
    ppermute x4, starting transfers between devices, send_x(): return lax.ppermute(x, 'tensor', pairs)  7.77 us
  transfers between devices with their start and end apart: 26, of which 5 were waited for; matrix products, arithmetic and copies ran while one was open for 0% of the time, Pallas kernels for 17%

profile of v1, /device:TPU:1, one launch (start us, length us, event | category | flops | bytes accessed | tf_op | source)
XLA Modules:
  0.0 121.0 jit_solution(12096053616136134009)
XLA Ops:
  0.6 0.0 copy-start
  0.6 1.4 %copy-done = f32[1,96,4096]{2,1,0:T(8,128)S(1)} copy-done((f32[1,96,4096]{2,1,0:T(8,128)S(1)}, f32[1,96,4096]{2,1,0:T(8,128)}, u32[]{:S(2)}) %copy-start) | copy-done | bytes 1572888
  2.0 0.1 shard_map.126
  2.2 3.3 %collective-permute-start.18 = (bf16[96,2048]{1,0:T(8,128)(2,1)S(1)}, bf16[96,2048]{1,0:T(8,128)(2,1)S(1)}, u32[]{:S(2)}, u32[]{:S(2)}) collective-permute-start(bf16[96,2048]{1,0:T(8,128)(2,1)S(1)} %shard_map.126), channel_id=1, source_target_pairs={{0,8},{8,0},{16,24},{24,16},{32,40},{40,32},{48,56},{56,48},{64,72... | collective-permute-start | bytes 1179656 | tf_op jit(solution)/shard_map/ppermute | solution.py:48
  5.5 1.3 %collective-permute-start.9 = (bf16[64,2560]{1,0:T(8,128)(2,1)S(1)}, bf16[64,2560]{1,0:T(8,128)(2,1)S(1)}, u32[]{:S(2)}, u32[]{:S(2)}) collective-permute-start(bf16[64,2560]{1,0:T(8,128)(2,1)S(1)} %slice.12), channel_id=1, source_target_pairs={{0,4},{1,5},{2,6},{3,7},{4,0},{5,1},{6,2},{7,3},{8,12},{9,13},{10,... | collective-permute-start | bytes 983048 | tf_op jit(solution)/shard_map/ppermute | solution.py:44
  6.8 1.4 %collective-permute-start.14 = (bf16[64,1536]{1,0:T(8,128)(2,1)S(1)}, bf16[64,1536]{1,0:T(8,128)(2,1)S(1)}, u32[]{:S(2)}, u32[]{:S(2)}) collective-permute-start(bf16[64,1536]{1,0:T(8,128)(2,1)S(1)} %slice.15), channel_id=1, source_target_pairs={{0,1},{1,2},{2,3},{3,0},{4,5},{5,6},{6,7},{7,4},{8,9},{9,10},{10,1... | collective-permute-start | bytes 589832 | tf_op jit(solution)/shard_map/ppermute | solution.py:39
  8.2 1.5 %collective-permute-start.15 = (bf16[64,1536]{1,0:T(8,128)(2,1)S(1)}, bf16[64,1536]{1,0:T(8,128)(2,1)S(1)}, u32[]{:S(2)}, u32[]{:S(2)}) collective-permute-start(bf16[64,1536]{1,0:T(8,128)(2,1)S(1)} %slice.15), channel_id=1, source_target_pairs={{0,3},{1,0},{2,1},{3,2},{4,7},{5,4},{6,5},{7,6},{8,11},{9,8},{10,9... | collective-permute-start | bytes 589832 | tf_op jit(solution)/shard_map/ppermute | solution.py:39
  9.7 7.4 %shard_map.118 = (bf16[64,2560]{1,0:T(8,128)(2,1)S(1)}, bf16[64,2560]{1,0:T(8,128)(2,1)S(1)}, bf16[128,2560]{1,0:T(8,128)(2,1)S(1)}, bf16[128,2560]{1,0:T(8,128)...) custom-call(bf16[512,512]{1,0:T(8,128)(2,1)S(1)} %copy-done.5, ...), custom_call_target="tpu_custom_call" | custom-call | flops 2147483648 | bytes 9437184 | tf_op jit(solution)/shard_map/pallas_call | solution.py:28
  17.1 0.1 collective-permute-start
  17.2 0.0 collective-permute-done.18.recv
  17.2 0.0 copy-start.3
  17.2 0.0 copy-start.4
  17.2 2.6 %collective-permute-start.2 = (bf16[64,2560]{1,0:T(8,128)(2,1)S(1)}, bf16[64,2560]{1,0:T(8,128)(2,1)S(1)}, u32[]{:S(2)}, u32[]{:S(2)}) collective-permute-start(bf16[64,2560]{1,0:T(8,128)(2,1)S(1)} %get-tuple-element.35), channel_id=1, source_target_pairs={{0,3},{1,0},{2,1},{3,2},{4,7},{5,4},{6,5},{7,6},{8,11},{9,8},{10,9... | collective-permute-start | bytes 983048 | tf_op jit(solution)/shard_map/ppermute | solution.py:39
  19.9 0.2 shard_map.127
  20.1 1.7 %collective-permute-start.5 = (bf16[256,1536]{1,0:T(8,128)(2,1)S(1)}, bf16[256,1536]{1,0:T(8,128)(2,1)S(1)}, u32[]{:S(2)}, u32[]{:S(2)}) collective-permute-start(bf16[256,1536]{1,0:T(8,128)(2,1)S(1)} %get-tuple-element.38), channel_id=1, source_target_pairs={{0,4},{1,5},{2,6},{3,7},{4,0},{5,1},{6,2},{7,3},{8,12},{9,13},{10,... | collective-permute-start | bytes 2359304 | tf_op jit(solution)/shard_map/ppermute | solution.py:44
  21.8 0.0 collective-permute-done.9
  21.9 19.6 %collective-permute-done.19.recv = bf16[96,1024]{1,0:T(8,128)(2,1)S(1)} collective-permute-done((bf16[96,1024]{1,0:T(8,128)(2,1)S(1)}, bf16[96,1024]{1,0:T(8,128)(2,1)S(1)}, u32[]{:S(2)}, u32[]{:S(2)}) %collective-permute-start.19) | collective-permute-done | bytes 196640 | tf_op jit(solution)/shard_map/ppermute | solution.py:48
  41.5 0.0 collective-permute-start.10
  41.5 0.1 shard_map.128
  41.5 0.0 collective-permute-done.15
  41.5 1.7 %collective-permute-start.20 = (bf16[96,1152]{1,0:T(8,128)(2,1)S(1)}, bf16[96,1152]{1,0:T(8,128)(2,1)S(1)}, u32[]{:S(2)}, u32[]{:S(2)}) collective-permute-start(bf16[96,1152]{1,0:T(8,128)(2,1)S(1)} %get-tuple-element.48.mine), channel_id=1, source_target_pairs={{0,32},{8,40},{16,48},{24,56},{32,0},{40,8},{48,16},{56,24},{64,96... | collective-permute-start | bytes 663560 | tf_op jit(solution)/shard_map/ppermute | solution.py:48
  43.3 3.3 %collective-permute-done.20.recv = bf16[96,1152]{1,0:T(8,128)(2,1)S(1)} collective-permute-done((bf16[96,1152]{1,0:T(8,128)(2,1)S(1)}, bf16[96,1152]{1,0:T(8,128)(2,1)S(1)}, u32[]{:S(2)}, u32[]{:S(2)}) %collective-permute-start.20) | collective-permute-done | bytes 221216 | tf_op jit(solution)/shard_map/ppermute | solution.py:48
  46.6 3.0 %collective-permute-start.11 = (bf16[128,2560]{1,0:T(8,128)(2,1)S(1)}, bf16[128,2560]{1,0:T(8,128)(2,1)S(1)}, u32[]{:S(2)}, u32[]{:S(2)}) collective-permute-start(bf16[128,2560]{1,0:T(8,128)(2,1)S(1)} %pad_maximum_fusion.1.x2), channel_id=1, source_target_pairs={{0,3},{1,0},{2,1},{3,2},{4,7},{5,4},{6,5},{7,6},{8,11},{9,8},{10,9... | collective-permute-start | bytes 1966088 | tf_op jit(solution)/shard_map/ppermute | solution.py:39
  49.6 0.1 shard_map.119
  49.6 0.1 shard_map.129
  49.7 0.0 collective-permute-done.2.r_ref
  49.7 0.1 collective-permute-start.1
  49.8 10.4 %collective-permute-done.16 = bf16[64,1536]{1,0:T(8,128)(2,1)S(1)} collective-permute-done((bf16[64,1536]{1,0:T(8,128)(2,1)S(1)}, bf16[64,1536]{1,0:T(8,128)(2,1)S(1)}, u32[]{:S(2)}, u32[]{:S(2)}) %collective-permute-start.16) | collective-permute-done | bytes 196640 | tf_op jit(solution)/shard_map/ppermute | solution.py:39
  60.3 3.0 %collective-permute-start.21 = (bf16[96,1280]{1,0:T(8,128)(2,1)S(1)}, bf16[96,1280]{1,0:T(8,128)(2,1)S(1)}, u32[]{:S(2)}, u32[]{:S(2)}) collective-permute-start(bf16[96,1280]{1,0:T(8,128)(2,1)S(1)} %get-tuple-element.50.mine), channel_id=1, source_target_pairs={{0,64},{8,72},{16,80},{24,88},{32,96},{40,104},{48,112},{56,120},{... | collective-permute-start | bytes 737288 | tf_op jit(solution)/shard_map/ppermute | solution.py:48
  63.3 0.1 pad_maximum_fusion.y4
  63.3 0.0 collective-permute-done.5.yx
  63.3 1.9 %collective-permute-start.17 = (bf16[256,1536]{1,0:T(8,128)(2,1)S(1)}, bf16[256,1536]{1,0:T(8,128)(2,1)S(1)}, u32[]{:S(2)}, u32[]{:S(2)}) collective-permute-start(bf16[256,1536]{1,0:T(8,128)(2,1)S(1)} %pad_maximum_fusion.y4), channel_id=1, source_target_pairs={{0,4},{1,5},{2,6},{3,7},{4,0},{5,1},{6,2},{7,3},{8,12},{9,13},{10,... | collective-permute-start | bytes 2359304 | tf_op jit(solution)/shard_map/ppermute | solution.py:44
  65.3 0.1 shard_map.120
  65.4 4.4 %collective-permute-done.21.recv = bf16[96,1280]{1,0:T(8,128)(2,1)S(1)} collective-permute-done((bf16[96,1280]{1,0:T(8,128)(2,1)S(1)}, bf16[96,1280]{1,0:T(8,128)(2,1)S(1)}, u32[]{:S(2)}, u32[]{:S(2)}) %collective-permute-start.21) | collective-permute-done | bytes 245792 | tf_op jit(solution)/shard_map/ppermute | solution.py:48
  69.8 0.0 collective-permute-start.3
  69.8 0.1 shard_map.130
  69.8 0.0 collective-permute-done.10.xm
  69.8 6.4 %collective-permute-start.22 = (bf16[96,1536]{1,0:T(8,128)(2,1)S(1)}, bf16[96,1536]{1,0:T(8,128)(2,1)S(1)}, u32[]{:S(2)}, u32[]{:S(2)}) collective-permute-start(bf16[96,1536]{1,0:T(8,128)(2,1)S(1)} %get-tuple-element.52.mine), channel_id=1, source_target_pairs={{0,128},{8,136},{16,144},{24,152},{32,160},{40,168},{48,176},{56,1... | collective-permute-start | bytes 884744 | tf_op jit(solution)/shard_map/ppermute | solution.py:48
  76.2 0.2 shard_map.122
  76.4 0.1 collective-permute-start.7
  76.6 1.5 %collective-permute-start.12 = (bf16[64,2560]{1,0:T(8,128)(2,1)S(1)}, bf16[64,2560]{1,0:T(8,128)(2,1)S(1)}, u32[]{:S(2)}, u32[]{:S(2)}) collective-permute-start(bf16[64,2560]{1,0:T(8,128)(2,1)S(1)} %slice.16), channel_id=1, source_target_pairs={{0,1},{1,2},{2,3},{3,0},{4,5},{5,6},{6,7},{7,4},{8,9},{9,10},{10,1... | collective-permute-start | bytes 983048 | tf_op jit(solution)/shard_map/ppermute | solution.py:39
  78.1 7.9 %collective-permute-done.22.recv = bf16[96,1536]{1,0:T(8,128)(2,1)S(1)} collective-permute-done((bf16[96,1536]{1,0:T(8,128)(2,1)S(1)}, bf16[96,1536]{1,0:T(8,128)(2,1)S(1)}, u32[]{:S(2)}, u32[]{:S(2)}) %collective-permute-start.22) | collective-permute-done | bytes 294944 | tf_op jit(solution)/shard_map/ppermute | solution.py:48
  86.0 0.0 collective-permute-start.13
  86.0 0.8 shard_map.131
  86.7 0.0 collective-permute-done.7.b
  86.7 0.3 collective-permute-start.24
  87.0 0.0 collective-permute-done.3.sm
  87.0 1.5 %collective-permute-start.6 = (bf16[64,1536]{1,0:T(8,128)(2,1)S(1)}, bf16[64,1536]{1,0:T(8,128)(2,1)S(1)}, u32[]{:S(2)}, u32[]{:S(2)}) collective-permute-start(bf16[64,1536]{1,0:T(8,128)(2,1)S(1)} %get-tuple-element.40), channel_id=1, source_target_pairs={{0,1},{1,2},{2,3},{3,0},{4,5},{5,6},{6,7},{7,4},{8,9},{9,10},{10,1... | collective-permute-start | bytes 589832 | tf_op jit(solution)/shard_map/ppermute | solution.py:39
  88.6 0.1 shard_map.121
  88.7 0.0 collective-permute-done.17.yx
  88.7 2.8 %collective-permute-start.4 = (bf16[64,2560]{1,0:T(8,128)(2,1)S(1)}, bf16[64,2560]{1,0:T(8,128)(2,1)S(1)}, u32[]{:S(2)}, u32[]{:S(2)}) collective-permute-start(bf16[64,2560]{1,0:T(8,128)(2,1)S(1)} %shard_map.121), channel_id=1, source_target_pairs={{0,4},{1,5},{2,6},{3,7},{4,0},{5,1},{6,2},{7,3},{8,12},{9,13},{10,... | collective-permute-start | bytes 983048 | tf_op jit(solution)/shard_map/ppermute | solution.py:44
  91.5 1.2 %collective-permute-start.8 = (bf16[64,1536]{1,0:T(8,128)(2,1)S(1)}, bf16[64,1536]{1,0:T(8,128)(2,1)S(1)}, u32[]{:S(2)}, u32[]{:S(2)}) collective-permute-start(bf16[64,1536]{1,0:T(8,128)(2,1)S(1)} %shard_map.123), channel_id=1, source_target_pairs={{0,3},{1,0},{2,1},{3,2},{4,7},{5,4},{6,5},{7,6},{8,11},{9,8},{10,9... | collective-permute-start | bytes 589832 | tf_op jit(solution)/shard_map/ppermute | solution.py:39
  92.8 0.0 collective-permute-done.13.f2
  92.8 15.7 %collective-permute-start.23 = (bf16[96,1024]{1,0:T(8,128)(2,1)S(1)}, bf16[96,1024]{1,0:T(8,128)(2,1)S(1)}, u32[]{:S(2)}, u32[]{:S(2)}) collective-permute-start(bf16[96,1024]{1,0:T(8,128)(2,1)S(1)} %get-tuple-element.53.q00), channel_id=1, source_target_pairs={{0,8},{8,0},{16,24},{24,16},{32,40},{40,32},{48,56},{56,48},{64,72... | collective-permute-start | bytes 589832 | tf_op jit(solution)/shard_map/ppermute | solution.py:48
  108.4 0.0 collective-permute-done.24.q10
  108.4 0.1 collective-permute-start.25
  108.5 10.0 %shard_map.125 = (bf16[512,4096]{1,0:T(8,128)(2,1)}, bf16[512,512]{1,0:T(8,128)(2,1)}) custom-call(bf16[512,512]{1,0:T(8,128)(2,1)S(1)} %copy-done.5, bf16[512,4096]{1,0:T(8,128)(2,1)} %bitcast.10, bf16[128,2560]{1,0:T(8,128)(2,1)S(1)} %pad_maximum_fusion.1.x2, bf16[128,2560]{1,0:T(8,128)(2,1)S(1)} %collective-permute-done.10.xm, ...), custom_call_target="tpu_custom_call" | custom-call | flops 4294967296 | bytes 14680064 | tf_op jit(solution)/shard_map/pallas_call | solution.py:28
  118.6 0.0 collective-permute-done.6.s1
  118.6 0.0 collective-permute-done.8.s2
  118.6 0.0 collective-permute-done.4.x
  118.6 0.0 copy-start.2
  118.6 1.0 shard_map.124
  119.6 0.1 copy-done.2
  119.7 1.3 %shard_map.132 = bf16[96,4096]{1,0:T(8,128)(2,1)} custom-call(bf16[96,4096]{1,0:T(8,128)(2,1)S(1)} %bitcast.7, bf16[96,1024]{1,0:T(8,128)(2,1)S(1)} %get-tuple-element.53.q00, bf16[96,1024]{1,0:T(8,128)(2,1)S(1)} %collective-permute-done.23.q01, bf16[96,1024]{1,0:T(8,128)(2,1)S(1)} %collective-permute-done.24.q10, ...), custom_call_target="tpu_custom_call" | custom-call | bytes 2359296 | tf_op jit(solution)/shard_map/pallas_call | solution.py:28
  (23 shorter events, 0.2 us)
Async XLA Ops:
  0.6 1.4 %copy-start = (f32[1,96,4096]{2,1,0:T(8,128)S(1)}, f32[1,96,4096]{2,1,0:T(8,128)}, u32[]{:S(2)}) copy-start(f32[1,96,4096]{2,1,0:T(8,128)} %param.10) | copy-start | bytes 4718596
  2.0 3.4 %copy-start.6 = (bf16[64,4096]{1,0:T(8,128)(2,1)S(1)}, bf16[64,4096]{1,0:T(8,128)(2,1)}, u32[]{:S(2)}) copy-start(bf16[64,4096]{1,0:T(8,128)(2,1)} %param.9) | copy-start | bytes 1572868
  2.0 7.6 %copy-start.5 = (bf16[512,512]{1,0:T(8,128)(2,1)S(1)}, bf16[512,512]{1,0:T(8,128)(2,1)}, u32[]{:S(2)}) copy-start(bf16[512,512]{1,0:T(8,128)(2,1)} %a_ref.3) | copy-start | bytes 1572868
  2.2 15.0 %collective-permute-start.18 = (bf16[96,2048]{1,0:T(8,128)(2,1)S(1)}, bf16[96,2048]{1,0:T(8,128)(2,1)S(1)}, u32[]{:S(2)}, u32[]{:S(2)}) collective-permute-start(bf16[96,2048]{1,0:T(8,128)(2,1)S(1)} %shard_map.126), channel_id=1, source_target_pairs={{0,8},{8,0},{16,24},{24,16},{32,40},{40,32},{48,56},{56,48},{64,72... | collective-permute-start | bytes 1179656 | tf_op jit(solution)/shard_map/ppermute | solution.py:48
  5.5 16.3 %collective-permute-start.9 = (bf16[64,2560]{1,0:T(8,128)(2,1)S(1)}, bf16[64,2560]{1,0:T(8,128)(2,1)S(1)}, u32[]{:S(2)}, u32[]{:S(2)}) collective-permute-start(bf16[64,2560]{1,0:T(8,128)(2,1)S(1)} %slice.12), channel_id=1, source_target_pairs={{0,4},{1,5},{2,6},{3,7},{4,0},{5,1},{6,2},{7,3},{8,12},{9,13},{10,... | collective-permute-start | bytes 983048 | tf_op jit(solution)/shard_map/ppermute | solution.py:44
  6.8 13.3 %collective-permute-start.14 = (bf16[64,1536]{1,0:T(8,128)(2,1)S(1)}, bf16[64,1536]{1,0:T(8,128)(2,1)S(1)}, u32[]{:S(2)}, u32[]{:S(2)}) collective-permute-start(bf16[64,1536]{1,0:T(8,128)(2,1)S(1)} %slice.15), channel_id=1, source_target_pairs={{0,1},{1,2},{2,3},{3,0},{4,5},{5,6},{6,7},{7,4},{8,9},{9,10},{10,1... | collective-permute-start | bytes 589832 | tf_op jit(solution)/shard_map/ppermute | solution.py:39
  8.2 33.4 %collective-permute-start.15 = (bf16[64,1536]{1,0:T(8,128)(2,1)S(1)}, bf16[64,1536]{1,0:T(8,128)(2,1)S(1)}, u32[]{:S(2)}, u32[]{:S(2)}) collective-permute-start(bf16[64,1536]{1,0:T(8,128)(2,1)S(1)} %slice.15), channel_id=1, source_target_pairs={{0,3},{1,0},{2,1},{3,2},{4,7},{5,4},{6,5},{7,6},{8,11},{9,8},{10,9... | collective-permute-start | bytes 589832 | tf_op jit(solution)/shard_map/ppermute | solution.py:39
  9.7 10.2 %copy-start.1 = (f32[1,96,4096]{2,1,0:T(8,128)S(1)}, f32[1,96,4096]{2,1,0:T(8,128)}, u32[]{:S(2)}) copy-start(f32[1,96,4096]{2,1,0:T(8,128)} %param.10) | copy-start | bytes 4718596
  17.1 26.2 %collective-permute-start = (bf16[64,2560]{1,0:T(8,128)(2,1)S(1)}, bf16[64,2560]{1,0:T(8,128)(2,1)S(1)}, u32[]{:S(2)}, u32[]{:S(2)}) collective-permute-start(bf16[64,2560]{1,0:T(8,128)(2,1)S(1)} %get-tuple-element.33), channel_id=1, source_target_pairs={{0,1},{1,2},{2,3},{3,0},{4,5},{5,6},{6,7},{7,4},{8,9},{9,10},{10,1... | collective-permute-start | bytes 983048 | tf_op jit(solution)/shard_map/ppermute | solution.py:39
  17.2 24.3 %copy-start.3 = (f32[96,128]{1,0:T(8,128)S(1)}, f32[96,128]{1,0:T(8,128)}, u32[]{:S(2)}) copy-start(f32[96,128]{1,0:T(8,128)} %glob.3) | copy-start | bytes 147460
  17.2 24.3 %copy-start.4 = (f32[96,128]{1,0:T(8,128)S(1)}, f32[96,128]{1,0:T(8,128)}, u32[]{:S(2)}) copy-start(f32[96,128]{1,0:T(8,128)} %mom.3) | copy-start | bytes 147460
  17.2 32.5 %collective-permute-start.2 = (bf16[64,2560]{1,0:T(8,128)(2,1)S(1)}, bf16[64,2560]{1,0:T(8,128)(2,1)S(1)}, u32[]{:S(2)}, u32[]{:S(2)}) collective-permute-start(bf16[64,2560]{1,0:T(8,128)(2,1)S(1)} %get-tuple-element.35), channel_id=1, source_target_pairs={{0,3},{1,0},{2,1},{3,2},{4,7},{5,4},{6,5},{7,6},{8,11},{9,8},{10,9... | collective-permute-start | bytes 983048 | tf_op jit(solution)/shard_map/ppermute | solution.py:39
  20.1 43.2 %collective-permute-start.5 = (bf16[256,1536]{1,0:T(8,128)(2,1)S(1)}, bf16[256,1536]{1,0:T(8,128)(2,1)S(1)}, u32[]{:S(2)}, u32[]{:S(2)}) collective-permute-start(bf16[256,1536]{1,0:T(8,128)(2,1)S(1)} %get-tuple-element.38), channel_id=1, source_target_pairs={{0,4},{1,5},{2,6},{3,7},{4,0},{5,1},{6,2},{7,3},{8,12},{9,13},{10,... | collective-permute-start | bytes 2359304 | tf_op jit(solution)/shard_map/ppermute | solution.py:44
  21.8 19.6 %collective-permute-start.19 = (bf16[96,1024]{1,0:T(8,128)(2,1)S(1)}, bf16[96,1024]{1,0:T(8,128)(2,1)S(1)}, u32[]{:S(2)}, u32[]{:S(2)}) collective-permute-start(bf16[96,1024]{1,0:T(8,128)(2,1)S(1)} %get-tuple-element.46), channel_id=1, source_target_pairs={{0,16},{8,24},{16,0},{24,8},{32,48},{40,56},{48,32},{56,40},{64,80... | collective-permute-start | bytes 589832 | tf_op jit(solution)/shard_map/ppermute | solution.py:48
  41.5 28.4 %collective-permute-start.10 = (bf16[128,2560]{1,0:T(8,128)(2,1)S(1)}, bf16[128,2560]{1,0:T(8,128)(2,1)S(1)}, u32[]{:S(2)}, u32[]{:S(2)}) collective-permute-start(bf16[128,2560]{1,0:T(8,128)(2,1)S(1)} %pad_maximum_fusion.1.x2), channel_id=1, source_target_pairs={{0,1},{1,2},{2,3},{3,0},{4,5},{5,6},{6,7},{7,4},{8,9},{9,10},{10,1... | collective-permute-start | bytes 1966088 | tf_op jit(solution)/shard_map/ppermute | solution.py:39
  41.5 5.0 %collective-permute-start.20 = (bf16[96,1152]{1,0:T(8,128)(2,1)S(1)}, bf16[96,1152]{1,0:T(8,128)(2,1)S(1)}, u32[]{:S(2)}, u32[]{:S(2)}) collective-permute-start(bf16[96,1152]{1,0:T(8,128)(2,1)S(1)} %get-tuple-element.48.mine), channel_id=1, source_target_pairs={{0,32},{8,40},{16,48},{24,56},{32,0},{40,8},{48,16},{56,24},{64,96... | collective-permute-start | bytes 663560 | tf_op jit(solution)/shard_map/ppermute | solution.py:48
  43.3 17.0 %collective-permute-start.16 = (bf16[64,1536]{1,0:T(8,128)(2,1)S(1)}, bf16[64,1536]{1,0:T(8,128)(2,1)S(1)}, u32[]{:S(2)}, u32[]{:S(2)}) collective-permute-start(bf16[64,1536]{1,0:T(8,128)(2,1)S(1)} %collective-permute-done.14), channel_id=1, source_target_pairs={{0,1},{1,2},{2,3},{3,0},{4,5},{5,6},{6,7},{7,4},{8,9},{9,10},{10,1... | collective-permute-start | bytes 589832 | tf_op jit(solution)/shard_map/ppermute | solution.py:39
  46.6 29.8 %collective-permute-start.11 = (bf16[128,2560]{1,0:T(8,128)(2,1)S(1)}, bf16[128,2560]{1,0:T(8,128)(2,1)S(1)}, u32[]{:S(2)}, u32[]{:S(2)}) collective-permute-start(bf16[128,2560]{1,0:T(8,128)(2,1)S(1)} %pad_maximum_fusion.1.x2), channel_id=1, source_target_pairs={{0,3},{1,0},{2,1},{3,2},{4,7},{5,4},{6,5},{7,6},{8,11},{9,8},{10,9... | collective-permute-start | bytes 1966088 | tf_op jit(solution)/shard_map/ppermute | solution.py:39
  49.7 26.8 %collective-permute-start.1 = (bf16[128,2560]{1,0:T(8,128)(2,1)S(1)}, bf16[128,2560]{1,0:T(8,128)(2,1)S(1)}, u32[]{:S(2)}, u32[]{:S(2)}) collective-permute-start(bf16[128,2560]{1,0:T(8,128)(2,1)S(1)} %shard_map.119), channel_id=1, source_target_pairs={{0,1},{1,2},{2,3},{3,0},{4,5},{5,6},{6,7},{7,4},{8,9},{9,10},{10,1... | collective-permute-start | bytes 1966088 | tf_op jit(solution)/shard_map/ppermute | solution.py:39
  60.3 9.5 %collective-permute-start.21 = (bf16[96,1280]{1,0:T(8,128)(2,1)S(1)}, bf16[96,1280]{1,0:T(8,128)(2,1)S(1)}, u32[]{:S(2)}, u32[]{:S(2)}) collective-permute-start(bf16[96,1280]{1,0:T(8,128)(2,1)S(1)} %get-tuple-element.50.mine), channel_id=1, source_target_pairs={{0,64},{8,72},{16,80},{24,88},{32,96},{40,104},{48,112},{56,120},{... | collective-permute-start | bytes 737288 | tf_op jit(solution)/shard_map/ppermute | solution.py:48
  63.3 25.4 %collective-permute-start.17 = (bf16[256,1536]{1,0:T(8,128)(2,1)S(1)}, bf16[256,1536]{1,0:T(8,128)(2,1)S(1)}, u32[]{:S(2)}, u32[]{:S(2)}) collective-permute-start(bf16[256,1536]{1,0:T(8,128)(2,1)S(1)} %pad_maximum_fusion.y4), channel_id=1, source_target_pairs={{0,4},{1,5},{2,6},{3,7},{4,0},{5,1},{6,2},{7,3},{8,12},{9,13},{10,... | collective-permute-start | bytes 2359304 | tf_op jit(solution)/shard_map/ppermute | solution.py:44
  69.8 17.3 %collective-permute-start.3 = (bf16[128,2560]{1,0:T(8,128)(2,1)S(1)}, bf16[128,2560]{1,0:T(8,128)(2,1)S(1)}, u32[]{:S(2)}, u32[]{:S(2)}) collective-permute-start(bf16[128,2560]{1,0:T(8,128)(2,1)S(1)} %shard_map.120), channel_id=1, source_target_pairs={{0,3},{1,0},{2,1},{3,2},{4,7},{5,4},{6,5},{7,6},{8,11},{9,8},{10,9... | collective-permute-start | bytes 1966088 | tf_op jit(solution)/shard_map/ppermute | solution.py:39
  69.8 16.1 %collective-permute-start.22 = (bf16[96,1536]{1,0:T(8,128)(2,1)S(1)}, bf16[96,1536]{1,0:T(8,128)(2,1)S(1)}, u32[]{:S(2)}, u32[]{:S(2)}) collective-permute-start(bf16[96,1536]{1,0:T(8,128)(2,1)S(1)} %get-tuple-element.52.mine), channel_id=1, source_target_pairs={{0,128},{8,136},{16,144},{24,152},{32,160},{40,168},{48,176},{56,1... | collective-permute-start | bytes 884744 | tf_op jit(solution)/shard_map/ppermute | solution.py:48
  76.4 10.3 %collective-permute-start.7 = (bf16[64,1536]{1,0:T(8,128)(2,1)S(1)}, bf16[64,1536]{1,0:T(8,128)(2,1)S(1)}, u32[]{:S(2)}, u32[]{:S(2)}) collective-permute-start(bf16[64,1536]{1,0:T(8,128)(2,1)S(1)} %get-tuple-element.42), channel_id=1, source_target_pairs={{0,3},{1,0},{2,1},{3,2},{4,7},{5,4},{6,5},{7,6},{8,11},{9,8},{10,9... | collective-permute-start | bytes 589832 | tf_op jit(solution)/shard_map/ppermute | solution.py:39
  76.6 15.0 %collective-permute-start.12 = (bf16[64,2560]{1,0:T(8,128)(2,1)S(1)}, bf16[64,2560]{1,0:T(8,128)(2,1)S(1)}, u32[]{:S(2)}, u32[]{:S(2)}) collective-permute-start(bf16[64,2560]{1,0:T(8,128)(2,1)S(1)} %slice.16), channel_id=1, source_target_pairs={{0,1},{1,2},{2,3},{3,0},{4,5},{5,6},{6,7},{7,4},{8,9},{9,10},{10,1... | collective-permute-start | bytes 983048 | tf_op jit(solution)/shard_map/ppermute | solution.py:39
  86.0 6.8 %collective-permute-start.13 = (bf16[64,2560]{1,0:T(8,128)(2,1)S(1)}, bf16[64,2560]{1,0:T(8,128)(2,1)S(1)}, u32[]{:S(2)}, u32[]{:S(2)}) collective-permute-start(bf16[64,2560]{1,0:T(8,128)(2,1)S(1)} %slice.17), channel_id=1, source_target_pairs={{0,3},{1,0},{2,1},{3,2},{4,7},{5,4},{6,5},{7,6},{8,11},{9,8},{10,9... | collective-permute-start | bytes 983048 | tf_op jit(solution)/shard_map/ppermute | solution.py:39
  86.7 21.7 %collective-permute-start.24 = (bf16[96,1024]{1,0:T(8,128)(2,1)S(1)}, bf16[96,1024]{1,0:T(8,128)(2,1)S(1)}, u32[]{:S(2)}, u32[]{:S(2)}) collective-permute-start(bf16[96,1024]{1,0:T(8,128)(2,1)S(1)} %get-tuple-element.53.q00), channel_id=1, source_target_pairs={{0,16},{8,24},{16,0},{24,8},{32,48},{40,56},{48,32},{56,40},{64,80... | collective-permute-start | bytes 589832 | tf_op jit(solution)/shard_map/ppermute | solution.py:48
  87.0 31.5 %collective-permute-start.6 = (bf16[64,1536]{1,0:T(8,128)(2,1)S(1)}, bf16[64,1536]{1,0:T(8,128)(2,1)S(1)}, u32[]{:S(2)}, u32[]{:S(2)}) collective-permute-start(bf16[64,1536]{1,0:T(8,128)(2,1)S(1)} %get-tuple-element.40), channel_id=1, source_target_pairs={{0,1},{1,2},{2,3},{3,0},{4,5},{5,6},{6,7},{7,4},{8,9},{9,10},{10,1... | collective-permute-start | bytes 589832 | tf_op jit(solution)/shard_map/ppermute | solution.py:39
  88.7 29.9 %collective-permute-start.4 = (bf16[64,2560]{1,0:T(8,128)(2,1)S(1)}, bf16[64,2560]{1,0:T(8,128)(2,1)S(1)}, u32[]{:S(2)}, u32[]{:S(2)}) collective-permute-start(bf16[64,2560]{1,0:T(8,128)(2,1)S(1)} %shard_map.121), channel_id=1, source_target_pairs={{0,4},{1,5},{2,6},{3,7},{4,0},{5,1},{6,2},{7,3},{8,12},{9,13},{10,... | collective-permute-start | bytes 983048 | tf_op jit(solution)/shard_map/ppermute | solution.py:44
  91.5 27.0 %collective-permute-start.8 = (bf16[64,1536]{1,0:T(8,128)(2,1)S(1)}, bf16[64,1536]{1,0:T(8,128)(2,1)S(1)}, u32[]{:S(2)}, u32[]{:S(2)}) collective-permute-start(bf16[64,1536]{1,0:T(8,128)(2,1)S(1)} %shard_map.123), channel_id=1, source_target_pairs={{0,3},{1,0},{2,1},{3,2},{4,7},{5,4},{6,5},{7,6},{8,11},{9,8},{10,9... | collective-permute-start | bytes 589832 | tf_op jit(solution)/shard_map/ppermute | solution.py:39
  92.8 26.8 %collective-permute-start.23 = (bf16[96,1024]{1,0:T(8,128)(2,1)S(1)}, bf16[96,1024]{1,0:T(8,128)(2,1)S(1)}, u32[]{:S(2)}, u32[]{:S(2)}) collective-permute-start(bf16[96,1024]{1,0:T(8,128)(2,1)S(1)} %get-tuple-element.53.q00), channel_id=1, source_target_pairs={{0,8},{8,0},{16,24},{24,16},{32,40},{40,32},{48,56},{56,48},{64,72... | collective-permute-start | bytes 589832 | tf_op jit(solution)/shard_map/ppermute | solution.py:48
  108.4 11.2 %collective-permute-start.25 = (bf16[96,1024]{1,0:T(8,128)(2,1)S(1)}, bf16[96,1024]{1,0:T(8,128)(2,1)S(1)}, u32[]{:S(2)}, u32[]{:S(2)}) collective-permute-start(bf16[96,1024]{1,0:T(8,128)(2,1)S(1)} %collective-permute-done.24.q10), channel_id=1, source_target_pairs={{0,8},{8,0},{16,24},{24,16},{32,40},{40,32},{48,56},{56,48},{64,72... | collective-permute-start | bytes 589832 | tf_op jit(solution)/shard_map/ppermute | solution.py:48
  118.6 1.1 copy-start.2

commit v2 on v0

v2 whole, which is shorter than its diff:
```python
import functools

import jax
import jax.numpy as jnp
from jax import lax
from jax.experimental import pallas as pl
from jax.experimental.pallas import tpu as pltpu
from jax.sharding import PartitionSpec as P

BF = jnp.bfloat16
F32 = jnp.float32
NY, NX = 4, 2
CX = 2560
CB = 512
LANE = 128
ORDER = (0, 3, 1, 2)
Y_LEFT, Y_RIGHT = slice(2560, 3328), slice(3328, 4096)
VMEM_LIMIT = 24 * 1024 * 1024


def call(kernel, outs, *args, deps=(), cost=None, **kw):
    if cost is None:
        size = sum(a.size * a.dtype.itemsize for a in (*args, *jax.tree.leaves(outs)))
        cost = pl.CostEstimate(flops=0, bytes_accessed=size, transcendentals=0)
    if "in_specs" not in kw:
        vmem = pl.BlockSpec(memory_space=pltpu.VMEM)
        kw.update(in_specs=[vmem] * len(args), out_specs=jax.tree.map(lambda _: vmem, outs))
    kw["in_specs"] = kw["in_specs"] + [pl.BlockSpec(memory_space=pl.ANY)] * len(deps)

    def body(*refs):
        kernel(*refs[: len(args)], *refs[len(args) + len(deps) :])

    return pl.pallas_call(
        body, out_shape=outs, cost_estimate=cost,
        compiler_params=pltpu.CompilerParams(vmem_limit_bytes=VMEM_LIMIT), **kw
    )(*args, *deps)


def sds(*shape, dtype=BF):
    return jax.ShapeDtypeStruct(shape, dtype)


def send_y(x, step):
    pairs = [(k * NY + y, k * NY + (y + step) % NY) for k in range(NX) for y in range(NY)]
    return lax.ppermute(x, "tensor", pairs)


def send_x(x):
    pairs = [(k * NY + y, (1 - k) * NY + y) for k in range(NX) for y in range(NY)]
    return lax.ppermute(x, "tensor", pairs)


def send_replica(x, bit):
    return lax.ppermute(x, "replica", [(r, r ^ bit) for r in range(lax.axis_size("replica"))])


def row_block(yi, xi):
    me = lax.axis_index("tensor")
    k, y = me // NY, me % NY
    return ((k + xi) % NX) * NY + (y + ORDER[yi]) % NY


def arrange_rows(a_ref, rel_ref):
    for yi in range(NY):
        for xi in range(NX):
            at = pl.multiple_of(row_block(yi, xi) * 64, 64)
            rel_ref[pl.ds((yi * NX + xi) * 64, 64), :] = a_ref[pl.ds(at, 64), :]


def blocks(first, last):
    return [slice(k, k + CB) for k in range(first, last, CB)]


def dot(x, y):
    return jnp.dot(x, y, preferred_element_type=F32).astype(BF)


def early_kernel(a_hbm, w_hbm, rel, w, p2a, p2b, py1, a, sems):
    d = w.shape[1]
    order = blocks(CX, d) + blocks(0, CX)
    copies = [pltpu.make_async_copy(a_hbm, a, sems.at[len(order)])]
    for i, k in enumerate(order):
        at = pl.ds(k.start, CB)
        copies.append(pltpu.make_async_copy(w_hbm.at[:, at], w.at[:, at], sems.at[i]))
    for copy in copies:
        copy.start()
    copies[0].wait()
    arrange_rows(a, rel)
    turned = jnp.concatenate([rel[yi * 128 + 64 : yi * 128 + 128, :] for yi in range(NY)], 0)
    for copy, k in zip(copies[1:], order):
        copy.wait()
        if k.start >= CX:
            py1[:, k.start - CX : k.stop - CX] = dot(turned, w[:, k])
        else:
            p = dot(rel[384:512, :], w[:, k])
            p2a[:, k] = p[0:64]
            p2b[:, k] = p[64:128]


def early(a, w, deps):
    d = w.shape[1]
    hbm, vmem = pl.BlockSpec(memory_space=pl.ANY), pl.BlockSpec(memory_space=pltpu.VMEM)
    return call(
        early_kernel,
        [sds(512, 512), sds(512, d), sds(64, CX), sds(64, CX), sds(256, d - CX)],
        a, w, deps=deps,
        in_specs=[hbm, hbm],
        out_specs=[vmem] * 5,
        scratch_shapes=[pltpu.VMEM((512, 512), BF), pltpu.SemaphoreType.DMA((d // CB + 1,))],
        cost=pl.CostEstimate(flops=0, bytes_accessed=12 << 20, transcendentals=0),
    )


def late_kernel(rel, w, p00, p01, pm, pp, py0):
    d = w.shape[1]
    for k in blocks(0, CX):
        p = dot(rel[0:384, :], w[:, k])
        p00[:, k] = p[0:64]
        p01[:, k] = p[64:128]
        pm[:, k] = p[128:256]
        pp[:, k] = p[256:384]
    kept = jnp.concatenate([rel[yi * 128 : yi * 128 + 64, :] for yi in range(NY)], 0)
    for k in blocks(CX, d):
        py0[:, k.start - CX : k.stop - CX] = dot(kept, w[:, k])


def grads_kernel(rel, w, gg, x1, ym, mu, yp, md, fu, fd, y4, yx, wg_hbm, hg, wg, g, sems):
    d = w.shape[1]
    across = rel[...].T
    copies = []
    for i, k in enumerate(blocks(0, d)):
        if k.start < CX:
            near, far = (slice(n * CX + k.start, n * CX + k.stop) for n in (1, 2))
            parts = (gg[:, k], x1[:, k], ym[:, k], mu[:, near], yp[:, k], md[:, near], fu[:, far], fd[:, far])
        else:
            cols = slice(k.start - CX, k.stop - CX)
            parts = [r[yi * 64 : yi * 64 + 64, cols] for yi in range(NY) for r in (y4, yx)]
        for n, p in enumerate(parts):
            g[n * 64 : n * 64 + 64, k] = p
        wg[:, k] = dot(across, g[:, k])
        at = pl.ds(k.start, CB)
        copies.append(pltpu.make_async_copy(wg.at[:, at], wg_hbm.at[:, at], sems.at[i]))
        copies[-1].start()
    h = lax.dot_general(
        g[...], w[...], (((1,), (1,)), ((), ())), preferred_element_type=F32
    ).astype(BF)
    for yi in range(NY):
        for xi in range(NX):
            at = pl.multiple_of(row_block(yi, xi) * 64, 64)
            n = (yi * NX + xi) * 64
            hg[pl.ds(at, 64), :] = h[n : n + 64]
    for copy in copies:
        copy.wait()


def grads(rel, w, *parts, deps):
    d = w.shape[1]
    hbm, vmem = pl.BlockSpec(memory_space=pl.ANY), pl.BlockSpec(memory_space=pltpu.VMEM)
    return call(
        grads_kernel,
        [sds(512, d), sds(512, 512)],
        rel, w, *parts, deps=deps,
        in_specs=[vmem] * (2 + len(parts)),
        out_specs=[hbm, vmem],
        scratch_shapes=[
            pltpu.VMEM((512, d), BF),
            pltpu.VMEM((512, d), BF),
            pltpu.SemaphoreType.DMA((d // CB,)),
        ],
        cost=pl.CostEstimate(flops=0, bytes_accessed=16 << 20, transcendentals=0),
    )


def f32(x):
    return x[...].astype(F32)


def copy_kernel(x, o):
    o[...] = x[...]


def core_split_kernel(d_ref, keep, send):
    _, _, c = bits()
    for i in range(send.shape[1] // LANE):
        keep[:, lanes(i)] = d_ref[:, lanes(2 * i + c)].astype(BF)
        send[:, lanes(i)] = d_ref[:, lanes(2 * i + 1 - c)].astype(BF)


def round2_kernel(p2a, p2b, x1, ym, yp, up, down):
    for out, p, y, cols in ((up, p2a, ym, Y_LEFT), (down, p2b, yp, Y_RIGHT)):
        out[:, 0:CX] = p[...]
        out[:, CX : 2 * CX] = x1[...]
        out[:, 2 * CX :] = y[:, cols]


def round3_kernel(pp, pm, mu, md, ym, g, yp, py0, yx, up, down, y4, q0, qp, qm):
    def q(yi):
        rows = slice(yi * 64, yi * 64 + 64)
        return f32(py0.at[rows, :]) + f32(yx.at[rows, :])

    q0[...] = q(0)
    qm[...] = q(1)
    qp[...] = q(2)
    q2 = q(3).astype(BF)
    half = (g.shape[1] - CX) // 2
    up[:, 0:CX] = (f32(pp.at[0:64, :]) + f32(mu.at[:, 0:CX])).astype(BF)
    up[:, CX : 2 * CX] = pp[64:128, :]
    up[:, 2 * CX : 3 * CX] = ym[:, 0:CX]
    up[:, 3 * CX :] = q2[:, 0:half]
    down[:, 0:CX] = pm[0:64, :]
    down[:, CX : 2 * CX] = (f32(pm.at[64:128, :]) + f32(md.at[:, 0:CX])).astype(BF)
    down[:, 2 * CX : 3 * CX] = md[:, CX : 2 * CX]
    down[:, 3 * CX :] = q2[:, half:]
    for i, r in enumerate((g, ym, yp)):
        y4[i * 64 : i * 64 + 64, :] = r[:, CX:]
    y4[192:256, 0:half] = mu[:, 2 * CX :]
    y4[192:256, half:] = md[:, 2 * CX :]


def round4_kernel(p01, fu, fd, qp, qm, up, down, x):
    half = qp.shape[1] // 2
    x[...] = (f32(p01) + f32(fu.at[:, CX : 2 * CX]) + f32(fd.at[:, CX : 2 * CX])).astype(BF)
    up[:, 0:half] = (qp[:, 0:half] + f32(fu.at[:, 3 * CX :])).astype(BF)
    up[:, half:] = qp[:, half:].astype(BF)
    down[:, 0:half] = qm[:, 0:half].astype(BF)
    down[:, half:] = (qm[:, half:] + f32(fd.at[:, 3 * CX :])).astype(BF)


def finish_kernel(p00, sp, sm, x, q0, s1, s2, o):
    o[:, 0:CX] = (
        f32(p00) + f32(sp.at[:, 0:CX]) + f32(sm.at[:, 0:CX]) + f32(x)
    ).astype(BF)
    o[:, CX:] = (f32(q0) + f32(s1) + f32(s2)).astype(BF)


def bits():
    r = lax.axis_index("replica")
    return r // 4, (r // 2) % 2, r % 2


def lanes(block):
    start = block * LANE
    return pl.ds(start if isinstance(start, int) else pl.multiple_of(start, LANE), LANE)


def core_add_kernel(mine, recv, keep, send):
    _, x, _ = bits()
    for i in range(keep.shape[1] // LANE):
        for out, k in ((send, 2 * i + 1 - x), (keep, 2 * i + x)):
            out[:, lanes(i)] = (f32(mine.at[:, lanes(k)]) + f32(recv.at[:, lanes(k)])).astype(out.dtype)


def x_add_kernel(keep, recv, glob, mom, total, send):
    n = keep.shape[1]
    t = f32(keep) + f32(recv)
    total[...] = t
    send[:, 0:n] = t.astype(BF)
    send[:, n:] = (glob[...] - 0.567 * mom[...]).astype(BF)


def z_bit(level):
    z, _, _ = bits()
    return (z // level) % 2


def z_add_kernel(level, keep, mine, recv, total, send):
    n = keep.shape[1]
    bit = z_bit(level)
    t = f32(keep) + f32(recv.at[:, 0:n])
    total[...] = t
    send[:, 0:n] = t.astype(BF)
    for i in range((mine.shape[1] - n) // LANE):
        send[:, lanes(n // LANE + 2 * i + bit)] = mine[:, lanes(n // LANE + i)]
        send[:, lanes(n // LANE + 2 * i + 1 - bit)] = recv[:, lanes(n // LANE + i)]


def update_kernel(replicas, level, keep, mine, recv, glob, mom, quarter, new_glob, new_mom):
    n = keep.shape[1]
    z, _, _ = bits()
    bit = z_bit(level)
    for src, side in ((mine, bit), (recv, 1 - bit)):
        for i in range((mine.shape[1] - n) // LANE):
            at = lanes(2 * i + side)
            mean = (keep[:, at] + f32(recv.at[:, at])) / replicas
            h = f32(src.at[:, lanes(n // LANE + i)])
            quarter[:, at] = (h - 1.33 * mean).astype(BF)
    at = lanes(z)
    mean = (keep[:, at] + f32(recv.at[:, at])) / replicas
    momentum = 0.9 * mom[...] + mean
    new_mom[...] = momentum
    new_glob[...] = glob[...] - 0.7 * (mean + 0.9 * momentum)


def merge_kernel(local, q00, q01, q10, q11, o):
    _, x, c = bits()
    for dx, dc, q in ((0, 0, q00), (0, 1, q01), (1, 0, q10), (1, 1, q11)):
        for i in range(q.shape[1] // LANE):
            xx = x + dx - 2 * x * dx
            cc = c + dc - 2 * c * dc
            at = lanes(4 * i + 2 * xx + cc)
            o[:, at] = (0.5 * f32(local.at[:, at]) + 0.5 * f32(q.at[:, lanes(i)])).astype(BF)


def on_device(
    head_outputs, output_weight, output_grad, outer_delta, local_slice, global_slice, momentum
):
    heads, weight, delta, local = head_outputs, output_weight[0], outer_delta[0], local_slice[0]
    replicas = lax.axis_size("replica")
    rows, d = delta.shape
    cy, n = d - CX, d // 4

    def part(fn, *fixed):
        return functools.partial(fn, *fixed)

    def f(*shape):
        return sds(*shape, dtype=F32)

    x1 = send_x(output_grad[:, :CX])
    ym = send_y(output_grad, 1)
    yp = send_y(output_grad, -1)
    keep, send = call(core_split_kernel, [sds(rows, d // 2)] * 2, delta)
    c1 = send_replica(send, 1)
    keep, send = call(core_add_kernel, [f(rows, n), sds(rows, n)], keep, c1)
    xl = send_replica(send, 2)

    rel, w, p2a, p2b, py1 = early(heads, weight, (send,))
    yx = send_x(py1)

    up, down = call(
        round2_kernel, [sds(64, 2 * CX + cy // 2)] * 2, p2a, p2b, x1, ym, yp, deps=(py1, xl)
    )
    mu, md = send_y(up, 1), send_y(down, -1)
    keep, mine = call(
        x_add_kernel, [f(rows, n), sds(rows, n + LANE)], keep, xl, global_slice, momentum, deps=(up,)
    )
    z4 = send_replica(mine, 16)
    p00, p01, pm, pp, py0 = call(
        late_kernel,
        [sds(64, CX), sds(64, CX), sds(128, CX), sds(128, CX), sds(256, cy)],
        rel, w, deps=(mine,),
        cost=pl.CostEstimate(flops=0, bytes_accessed=8 << 20, transcendentals=0),
    )
    keep, mine = call(
        part(z_add_kernel, 4), [f(rows, n), sds(rows, n + 2 * LANE)], keep, mine, z4, deps=(py0,)
    )
    z2 = send_replica(mine, 8)

    up, down, y4, q0, qp, qm = call(
        round3_kernel,
        [sds(64, 3 * CX + cy // 2)] * 2 + [sds(256, cy)] + [f(64, cy)] * 3,
        pp, pm, mu, md, ym, output_grad, yp, py0, yx, deps=(mine,),
    )
    fu, fd = send_y(up, 1), send_y(down, -1)
    gyx = send_x(y4)
    keep, mine = call(
        part(z_add_kernel, 2), [f(rows, n), sds(rows, n + 4 * LANE)], keep, mine, z2, deps=(y4,)
    )
    z1 = send_replica(mine, 4)
    q00, new_global, new_momentum = call(
        part(update_kernel, replicas, 1), [sds(rows, n), f(*momentum.shape), f(*momentum.shape)],
        keep, mine, z1, global_slice, momentum,
    )
    q01 = send_replica(q00, 1)
    q10 = call(copy_kernel, sds(rows, n), send_replica(q00, 2))
    q11 = send_replica(q10, 1)

    up, down, x = call(
        round4_kernel, [sds(64, cy), sds(64, cy), sds(64, CX)], p01, fu, fd, qp, qm, deps=(q10,)
    )
    s1, s2 = send_y(up, 1), send_y(down, -1)
    x = send_x(x)
    weight_grad, head_grads = grads(
        rel, w, output_grad, x1, ym, mu, yp, md, fu, fd, y4, gyx, deps=(up,)
    )
    merged = call(merge_kernel, sds(rows, d), local, q00, q01, q10, q11, deps=(head_grads,))
    projected = call(finish_kernel, sds(64, d), p00, fu, fd, x, q0, s1, s2, deps=(merged,))
    return (projected, head_grads, weight_grad[None], merged[None], new_global, new_momentum)


def solution(mesh):
    in_specs = (
        P("replica", "tensor"),
        P("replica", "tensor", None),
        P(("replica", "tensor"), None),
        P("replica", "tensor", None),
        P("replica", "tensor", None),
        P("tensor", "replica"),
        P("tensor", "replica"),
    )
    out_specs = (
        P(("replica", "tensor"), None),
        P("replica", "tensor"),
        P("replica", "tensor", None),
        P("replica", "tensor", None),
        P("tensor", "replica"),
        P("tensor", "replica"),
    )
    return jax.shard_map(
        on_device, mesh=mesh, in_specs=in_specs, out_specs=out_specs, check_vma=False
    )
```

time: 251 us -> 86.2 us (0.34)
  waiting for transfers between devices: 174 us -> 29.2 us
  blocking collectives: 36 us -> 0 us
  starting transfers between devices: 0.12 us -> 35 us
  matrix products: 16.4 us -> 0 us
  Pallas kernels: 0 us -> 15.1 us
  between operations: 15.5 us -> 0.83 us
  other arithmetic: 3.31 us -> 0 us
    unnamed x4 -> x0, waiting for transfers between devices: 127 us -> none
    reduce_scatter x1 -> x0, waiting for transfers between devices: 47.6 us -> none  [layer_work(): lax.psum_scatter(jnp.dot(block, weight, preferred_element_type=jnp.float3...]
    all_gather x1 -> x0, blocking collectives: 36 us -> none  [outer_work(): lax.all_gather(new_global.astype(jnp.bfloat16), 'replica', axis=1, tiled=...]
    ppermute x0 -> x20, starting transfers between devices: none -> 35 us  [the longest x8 18 us: send_replica(): lax.ppermute(x, 'replica', [(r, r ^ bit) for r in range(lax.axis_size('re...]
    ppermute x0 -> x20, waiting for transfers between devices: none -> 29.2 us  [the longest x8 21.2 us: send_replica(): lax.ppermute(x, 'replica', [(r, r ^ bit) for r in range(lax.axis_size('re...]
    dot_general x3 -> x0, matrix products: 16.4 us -> none  [the longest x1 6.75 us: layer_work(): lax.dot_general(block, shard_rows, (((0,), (0,)), ((), ())), preferred_el...]
    pallas_call x0 -> x15, Pallas kernels: none -> 15.1 us  [call(): pl.pallas_call(body, out_shape=outs, cost_estimate=cost, compiler_params=...]
    unnamed x16 -> x18, local copies, waits for them, and re-layouts: 4.83 us -> 5.84 us
  transfers between devices with their start and end apart: 3 -> 20, of which waited for: 2 -> 8; matrix products, arithmetic and copies ran while one was open for 8% -> 0% of each run, Pallas kernels for 0% -> 16%
where the time goes in v2:
time: 86.2 us; the launch traced here: 86 us
  starting transfers between devices  35 us (41%)
  waiting for transfers between devices  29.2 us (34%)
  Pallas kernels  15.1 us (18%)
  local copies, waits for them, and re-layouts  5.86 us (7%)
    ppermute x8, waiting for transfers between devices, send_replica(): lax.ppermute(x, 'replica', [(r, r ^ bit) for r in range(lax.axis_size('re...  21.2 us
    ppermute x8, starting transfers between devices, send_replica(): lax.ppermute(x, 'replica', [(r, r ^ bit) for r in range(lax.axis_size('re...  18 us
    pallas_call x15, Pallas kernels, call(): pl.pallas_call(body, out_shape=outs, cost_estimate=cost, compiler_params=...  15.1 us
    ppermute x8, starting transfers between devices, send_y(): return lax.ppermute(x, 'tensor', pairs)  9.66 us
    ppermute x4, starting transfers between devices, send_x(): return lax.ppermute(x, 'tensor', pairs)  7.33 us
    ppermute x4, waiting for transfers between devices, send_x(): return lax.ppermute(x, 'tensor', pairs)  6.15 us
    unnamed x18, local copies, waits for them, and re-layouts  5.84 us
    ppermute x8, waiting for transfers between devices, send_y(): return lax.ppermute(x, 'tensor', pairs)  1.78 us
  transfers between devices with their start and end apart: 20, of which 8 were waited for; matrix products, arithmetic and copies ran while one was open for 0% of the time, Pallas kernels for 16%

profile of v2, /device:TPU:1, one launch (start us, length us, event | category | flops | bytes accessed | tf_op | source)
XLA Modules:
  0.0 86.0 jit_solution(11079486481689946890)
XLA Ops:
  0.6 0.0 copy-start.1
  0.7 1.5 %copy-done.3 = f32[1,96,4096]{2,1,0:T(8,128)S(1)} copy-done((f32[1,96,4096]{2,1,0:T(8,128)S(1)}, f32[1,96,4096]{2,1,0:T(8,128)}, u32[]{:S(2)}) %copy-start.3) | copy-done | bytes 1572888
  2.1 0.2 shard_map.118
  2.3 3.3 %collective-permute-start = (bf16[96,2048]{1,0:T(8,128)(2,1)S(1)}, bf16[96,2048]{1,0:T(8,128)(2,1)S(1)}, u32[]{:S(2)}, u32[]{:S(2)}) collective-permute-start(bf16[96,2048]{1,0:T(8,128)(2,1)S(1)} %get-tuple-element.43), channel_id=1, source_target_pairs={{0,8},{8,0},{16,24},{24,16},{32,40},{40,32},{48,56},{56,48},{64,72... | collective-permute-start | bytes 1179656 | tf_op jit(solution)/shard_map/ppermute | solution.py:54
  5.7 0.0 collective-permute-start.3
  5.7 2.7 %collective-permute-start.4 = (bf16[64,4096]{1,0:T(8,128)(2,1)S(1)}, bf16[64,4096]{1,0:T(8,128)(2,1)S(1)}, u32[]{:S(2)}, u32[]{:S(2)}) collective-permute-start(bf16[64,4096]{1,0:T(8,128)(2,1)S(1)} %copy-done.1), channel_id=1, source_target_pairs={{0,3},{1,0},{2,1},{3,2},{4,7},{5,4},{6,5},{7,6},{8,11},{9,8},{10,9... | collective-permute-start | bytes 1572872 | tf_op jit(solution)/shard_map/ppermute | solution.py:45
  8.4 1.1 %collective-permute-start.2 = (bf16[64,2560]{1,0:T(8,128)(2,1)S(1)}, bf16[64,2560]{1,0:T(8,128)(2,1)S(1)}, u32[]{:S(2)}, u32[]{:S(2)}) collective-permute-start(bf16[64,2560]{1,0:T(8,128)(2,1)S(1)} %slice.3), channel_id=1, source_target_pairs={{0,4},{1,5},{2,6},{3,7},{4,0},{5,1},{6,2},{7,3},{8,12},{9,13},{10,... | collective-permute-start | bytes 983048 | tf_op jit(solution)/shard_map/ppermute | solution.py:50
  9.5 0.0 collective-permute-done.refs_1_
  9.5 0.2 shard_map.119
  9.7 0.4 collective-permute-start.1
  10.1 2.2 %copy-done = bf16[1,512,4096]{2,1,0:T(8,128)(2,1)S(1)} copy-done((bf16[1,512,4096]{2,1,0:T(8,128)(2,1)S(1)}, bf16[1,512,4096]{2,1,0:T(8,128)(2,1)}, u32[]{:S(2)}) %copy-start) | copy-done | bytes 4194328
  12.3 3.3 %shard_map.120 = (bf16[512,512]{1,0:T(8,128)(2,1)S(1)}, bf16[512,4096]{1,0:T(8,128)(2,1)S(1)}, bf16[64,2560]{1,0:T(8,128)(2,1)S(1)}, bf16[64,2560]{1,0:T(8,128)(2,1)S(1)}, bf16[256,1536]{1,0:T(8,128)(2,1)S(1)}) custom-call(bf16[512,512]{1,0:T(8,128)(2,1)S(1)} %copy-done.5, bf16[512,4096]{1,0:T(8,128)(2,1)S(1)} %bitcast.5, ...), custom_call_target="tpu_custom_call" | custom-call | bytes 12582912 | tf_op jit(solution)/shard_map/pallas_call | solution.py:33
  15.6 0.0 copy-start.7
  15.6 0.0 copy-start.8
  15.6 1.8 %collective-permute-start.7 = (bf16[256,1536]{1,0:T(8,128)(2,1)S(1)}, bf16[256,1536]{1,0:T(8,128)(2,1)S(1)}, u32[]{:S(2)}, u32[]{:S(2)}) collective-permute-start(bf16[256,1536]{1,0:T(8,128)(2,1)S(1)} %get-tuple-element.50.refs_5_), channel_id=1, source_target_pairs={{0,4},{1,5},{2,6},{3,7},{4,0},{5,1},{6,2},{7,3},{8,12},{9,13},{10,... | collective-permute-start | bytes 2359304 | tf_op jit(solution)/shard_map/ppermute | solution.py:50
  17.4 1.1 %collective-permute-done.2.refs_2_.refs_3_ = bf16[64,2560]{1,0:T(8,128)(2,1)S(1)} collective-permute-done((bf16[64,2560]{1,0:T(8,128)(2,1)S(1)}, bf16[64,2560]{1,0:T(8,128)(2,1)S(1)}, u32[]{:S(2)}, u32[]{:S(2)}) %collective-permute-start.2) | collective-permute-done | bytes 327712 | tf_op jit(solution)/shard_map/ppermute | solution.py:50
  18.6 1.8 %collective-permute-done.3.refs_3_.refs_4_ = bf16[64,4096]{1,0:T(8,128)(2,1)S(1)} collective-permute-done((bf16[64,4096]{1,0:T(8,128)(2,1)S(1)}, bf16[64,4096]{1,0:T(8,128)(2,1)S(1)}, u32[]{:S(2)}, u32[]{:S(2)}) %collective-permute-start.3) | collective-permute-done | bytes 524320 | tf_op jit(solution)/shard_map/ppermute | solution.py:45
  20.3 0.0 collective-permute-done.4.refs_4_.refs_6_
  20.4 0.9 %collective-permute-done.1.refs_6_.refs_1_ = bf16[96,1024]{1,0:T(8,128)(2,1)S(1)} collective-permute-done((bf16[96,1024]{1,0:T(8,128)(2,1)S(1)}, bf16[96,1024]{1,0:T(8,128)(2,1)S(1)}, u32[]{:S(2)}, u32[]{:S(2)}) %collective-permute-start.1) | collective-permute-done | bytes 196640 | tf_op jit(solution)/shard_map/ppermute | solution.py:54
  21.2 0.1 shard_map.121
  21.3 0.1 collective-permute-start.5
  21.4 2.7 %collective-permute-start.6 = (bf16[64,5888]{1,0:T(8,128)(2,1)S(1)}, bf16[64,5888]{1,0:T(8,128)(2,1)S(1)}, u32[]{:S(2)}, u32[]{:S(2)}) collective-permute-start(bf16[64,5888]{1,0:T(8,128)(2,1)S(1)} %get-tuple-element.56), channel_id=1, source_target_pairs={{0,3},{1,0},{2,1},{3,2},{4,7},{5,4},{6,5},{7,6},{8,11},{9,8},{10,9... | collective-permute-start | bytes 2261000 | tf_op jit(solution)/shard_map/ppermute | solution.py:45
  24.1 0.0 copy-done.8
  24.1 0.1 shard_map.122
  24.2 7.0 %collective-permute-start.8 = (bf16[96,1152]{1,0:T(8,128)(2,1)S(1)}, bf16[96,1152]{1,0:T(8,128)(2,1)S(1)}, u32[]{:S(2)}, u32[]{:S(2)}) collective-permute-start(bf16[96,1152]{1,0:T(8,128)(2,1)S(1)} %get-tuple-element.52.refs_2_.refs_1_), channel_id=1, source_target_pairs={{0,128},{8,136},{16,144},{24,152},{32,160},{40,168},{48,176},{56,1... | collective-permute-start | bytes 663560 | tf_op jit(solution)/shard_map/ppermute | solution.py:54
  31.2 1.6 %shard_map.123 = (bf16[64,2560]{1,0:T(8,128)(2,1)S(1)}, bf16[64,2560]{1,0:T(8,128)(2,1)S(1)}, bf16[128,2560]{1,0:T(8,128)(2,1)S(1)}, bf16[128,2560]{1,0:T(8,128)(2,1)S(1)}, bf16[256,1536]{1,0:T(8,128)(2,1)S(1)}) custom-call(bf16[512,512]{1,0:T(8,128)(2,1)S(1)} %get-tuple-element.45.refs_0_, bf16[512,4096]{1,0:T(8,128)(2,1)S(1)} %get-tuple-element.46.refs_1_, ...), custom_call_target="tpu_custom_call" | custom-call | bytes 8388608 | tf_op jit(solution)/shard_map/pallas_call | solution.py:33
  32.8 1.8 %collective-permute-done.8.refs_2_ = bf16[96,1152]{1,0:T(8,128)(2,1)S(1)} collective-permute-done((bf16[96,1152]{1,0:T(8,128)(2,1)S(1)}, bf16[96,1152]{1,0:T(8,128)(2,1)S(1)}, u32[]{:S(2)}, u32[]{:S(2)}) %collective-permute-start.8) | collective-permute-done | bytes 221216 | tf_op jit(solution)/shard_map/ppermute | solution.py:54
  34.6 0.1 shard_map.124
  34.6 5.0 %collective-permute-done.7.refs_8_ = bf16[256,1536]{1,0:T(8,128)(2,1)S(1)} collective-permute-done((bf16[256,1536]{1,0:T(8,128)(2,1)S(1)}, bf16[256,1536]{1,0:T(8,128)(2,1)S(1)}, u32[]{:S(2)}, u32[]{:S(2)}) %collective-permute-start.7) | collective-permute-done | bytes 786464 | tf_op jit(solution)/shard_map/ppermute | solution.py:50
  39.6 0.0 collective-permute-done.5.refs_2_.refs_5_
  39.7 0.0 collective-permute-done.6.refs_3_.refs_7_
  39.7 0.4 shard_map.125
  40.0 1.3 %collective-permute-start.10 = (bf16[64,8448]{1,0:T(8,128)(2,1)S(1)}, bf16[64,8448]{1,0:T(8,128)(2,1)S(1)}, u32[]{:S(2)}, u32[]{:S(2)}) collective-permute-start(bf16[64,8448]{1,0:T(8,128)(2,1)S(1)} %get-tuple-element.61), channel_id=1, source_target_pairs={{0,3},{1,0},{2,1},{3,2},{4,7},{5,4},{6,5},{7,6},{8,11},{9,8},{10,9... | collective-permute-start | bytes 3244040 | tf_op jit(solution)/shard_map/ppermute | solution.py:45
  41.3 0.3 collective-permute-start.9
  41.6 2.7 %collective-permute-start.11 = (bf16[96,1280]{1,0:T(8,128)(2,1)S(1)}, bf16[96,1280]{1,0:T(8,128)(2,1)S(1)}, u32[]{:S(2)}, u32[]{:S(2)}) collective-permute-start(bf16[96,1280]{1,0:T(8,128)(2,1)S(1)} %get-tuple-element.59.refs_9_.refs_1_), channel_id=1, source_target_pairs={{0,64},{8,72},{16,80},{24,88},{32,96},{40,104},{48,112},{56,120},{... | collective-permute-start | bytes 737288 | tf_op jit(solution)/shard_map/ppermute | solution.py:54
  44.3 1.7 %collective-permute-start.19 = (bf16[256,1536]{1,0:T(8,128)(2,1)S(1)}, bf16[256,1536]{1,0:T(8,128)(2,1)S(1)}, u32[]{:S(2)}, u32[]{:S(2)}) collective-permute-start(bf16[256,1536]{1,0:T(8,128)(2,1)S(1)} %get-tuple-element.66.refs_3_.refs_10_), channel_id=1, source_target_pairs={{0,4},{1,5},{2,6},{3,7},{4,0},{5,1},{6,2},{7,3},{8,12},{9,13},{10,... | collective-permute-start | bytes 2359304 | tf_op jit(solution)/shard_map/ppermute | solution.py:50
  46.0 8.4 %collective-permute-done.11.refs_2_ = bf16[96,1280]{1,0:T(8,128)(2,1)S(1)} collective-permute-done((bf16[96,1280]{1,0:T(8,128)(2,1)S(1)}, bf16[96,1280]{1,0:T(8,128)(2,1)S(1)}, u32[]{:S(2)}, u32[]{:S(2)}) %collective-permute-start.11) | collective-permute-done | bytes 245792 | tf_op jit(solution)/shard_map/ppermute | solution.py:54
  54.5 0.1 shard_map.126
  54.5 0.2 collective-permute-start.12
  54.7 6.4 %collective-permute-done.12.refs_2_ = bf16[96,1536]{1,0:T(8,128)(2,1)S(1)} collective-permute-done((bf16[96,1536]{1,0:T(8,128)(2,1)S(1)}, bf16[96,1536]{1,0:T(8,128)(2,1)S(1)}, u32[]{:S(2)}, u32[]{:S(2)}) %collective-permute-start.12) | collective-permute-done | bytes 294944 | tf_op jit(solution)/shard_map/ppermute | solution.py:54
  61.1 0.7 shard_map.127
  61.9 1.2 %collective-permute-start.13 = (bf16[96,1024]{1,0:T(8,128)(2,1)S(1)}, bf16[96,1024]{1,0:T(8,128)(2,1)S(1)}, u32[]{:S(2)}, u32[]{:S(2)}) collective-permute-start(bf16[96,1024]{1,0:T(8,128)(2,1)S(1)} %get-tuple-element.69.refs_1_), channel_id=1, source_target_pairs={{0,16},{8,24},{16,0},{24,8},{32,48},{40,56},{48,32},{56,40},{64,80... | collective-permute-start | bytes 589832 | tf_op jit(solution)/shard_map/ppermute | solution.py:54
  63.0 3.7 %collective-permute-done.13.refs_0_ = bf16[96,1024]{1,0:T(8,128)(2,1)S(1)} collective-permute-done((bf16[96,1024]{1,0:T(8,128)(2,1)S(1)}, bf16[96,1024]{1,0:T(8,128)(2,1)S(1)}, u32[]{:S(2)}, u32[]{:S(2)}) %collective-permute-start.13) | collective-permute-done | bytes 196640 | tf_op jit(solution)/shard_map/ppermute | solution.py:54
  66.7 0.0 collective-permute-done.10.refs_2_.refs_9_
  66.7 0.0 collective-permute-done.9.refs_1_.refs_8_
  66.7 0.2 shard_map.129
  66.9 2.6 %collective-permute-start.14 = (bf16[64,2560]{1,0:T(8,128)(2,1)S(1)}, bf16[64,2560]{1,0:T(8,128)(2,1)S(1)}, u32[]{:S(2)}, u32[]{:S(2)}) collective-permute-start(bf16[64,2560]{1,0:T(8,128)(2,1)S(1)} %get-tuple-element.70), channel_id=1, source_target_pairs={{0,4},{1,5},{2,6},{3,7},{4,0},{5,1},{6,2},{7,3},{8,12},{9,13},{10,... | collective-permute-start | bytes 983048 | tf_op jit(solution)/shard_map/ppermute | solution.py:50
  69.5 3.2 %collective-permute-start.17 = (bf16[96,1024]{1,0:T(8,128)(2,1)S(1)}, bf16[96,1024]{1,0:T(8,128)(2,1)S(1)}, u32[]{:S(2)}, u32[]{:S(2)}) collective-permute-start(bf16[96,1024]{1,0:T(8,128)(2,1)S(1)} %get-tuple-element.69.refs_1_), channel_id=1, source_target_pairs={{0,8},{8,0},{16,24},{24,16},{32,40},{40,32},{48,56},{56,48},{64,72... | collective-permute-start | bytes 589832 | tf_op jit(solution)/shard_map/ppermute | solution.py:54
  72.8 0.0 collective-permute-start.18
  72.8 0.1 collective-permute-start.15
  72.9 0.0 collective-permute-done.19.refs_11_
  72.9 2.6 %collective-permute-start.16 = (bf16[64,1536]{1,0:T(8,128)(2,1)S(1)}, bf16[64,1536]{1,0:T(8,128)(2,1)S(1)}, u32[]{:S(2)}, u32[]{:S(2)}) collective-permute-start(bf16[64,1536]{1,0:T(8,128)(2,1)S(1)} %get-tuple-element.73), channel_id=1, source_target_pairs={{0,3},{1,0},{2,1},{3,2},{4,7},{5,4},{6,5},{7,6},{8,11},{9,8},{10,9... | collective-permute-start | bytes 589832 | tf_op jit(solution)/shard_map/ppermute | solution.py:45
  75.5 5.9 %shard_map.130 = (bf16[512,4096]{1,0:T(8,128)(2,1)}, bf16[512,512]{1,0:T(8,128)(2,1)}) custom-call(bf16[512,512]{1,0:T(8,128)(2,1)S(1)} %get-tuple-element.45.refs_0_, bf16[512,4096]{1,0:T(8,128)(2,1)S(1)} %get-tuple-element.46.refs_1_, bf16[64,4096]{1,0:T(8,128)(2,1)S(1)} %copy-done.1, bf16[64,2560]{1,0:T(8,128)(2,1)S(1)} %collective-permute-done.2.refs_2_.refs_3_, ...), custom_call_target="tpu_custom_call" | custom-call | bytes 16777216 | tf_op jit(solution)/shard_map/pallas_call | solution.py:33
  81.4 0.0 collective-permute-done.17.refs_2_
  81.4 0.0 collective-permute-done.18.refs_4_
  81.4 0.0 copy-start.6
  81.4 1.0 %copy-done.6 = bf16[512,512]{1,0:T(8,128)(2,1)S(1)} copy-done((bf16[512,512]{1,0:T(8,128)(2,1)S(1)}, bf16[512,512]{1,0:T(8,128)(2,1)}, u32[]{:S(2)}) %copy-start.6) | copy-done | bytes 524312
  82.5 1.3 %shard_map.131.refs_7_ = bf16[96,4096]{1,0:T(8,128)(2,1)} custom-call(bf16[96,4096]{1,0:T(8,128)(2,1)S(1)} %bitcast.8, bf16[96,1024]{1,0:T(8,128)(2,1)S(1)} %get-tuple-element.69.refs_1_, bf16[96,1024]{1,0:T(8,128)(2,1)S(1)} %collective-permute-done.17.refs_2_, bf16[96,1024]{1,0:T(8,128)(2,1)S(1)} %shard_map.128.refs_5_.refs_3_, ...), custom_call_target="tpu_custom_call" | custom-call | bytes 2359296 | tf_op jit(solution)/shard_map/pallas_call | solution.py:33
  83.8 0.0 collective-permute-done.15.refs_5_
  83.8 0.0 collective-permute-done.16.refs_6_
  83.8 0.0 collective-permute-done.14.refs_3_
  83.8 0.0 copy-start.2
  83.8 1.1 %copy-done.2 = bf16[96,4096]{1,0:T(8,128)(2,1)S(1)} copy-done((bf16[96,4096]{1,0:T(8,128)(2,1)S(1)}, bf16[96,4096]{1,0:T(8,128)(2,1)}, u32[]{:S(2)}) %copy-start.2) | copy-done | bytes 786456
  84.9 1.0 %shard_map.132 = bf16[64,4096]{1,0:T(8,128)(2,1)} custom-call(bf16[64,2560]{1,0:T(8,128)(2,1)S(1)} %get-tuple-element.53.refs_0_, bf16[64,8448]{1,0:T(8,128)(2,1)S(1)} %collective-permute-done.9.refs_1_.refs_8_, bf16[64,8448]{1,0:T(8,128)(2,1)S(1)} %collective-permute-done.10.refs_2_.refs_9_, bf16[64,2560]{1,0:T(8,128)(2,1)S(1)} %collective-permute-done.14.refs_3_, ...), custom_call_target="tpu_custom_call" | custom-call | bytes 4128768 | tf_op jit(solution)/shard_map/pallas_call | solution.py:33
  (10 shorter events, 0.1 us)
Async XLA Ops:
  0.6 5.0 %copy-start.1 = (bf16[64,4096]{1,0:T(8,128)(2,1)S(1)}, bf16[64,4096]{1,0:T(8,128)(2,1)}, u32[]{:S(2)}) copy-start(bf16[64,4096]{1,0:T(8,128)(2,1)} %refs_2_.3) | copy-start | bytes 1572868
  0.6 1.5 %copy-start.3 = (f32[1,96,4096]{2,1,0:T(8,128)S(1)}, f32[1,96,4096]{2,1,0:T(8,128)}, u32[]{:S(2)}) copy-start(f32[1,96,4096]{2,1,0:T(8,128)} %param.10) | copy-start | bytes 4718596
  2.1 8.0 %copy-start.5 = (bf16[512,512]{1,0:T(8,128)(2,1)S(1)}, bf16[512,512]{1,0:T(8,128)(2,1)}, u32[]{:S(2)}) copy-start(bf16[512,512]{1,0:T(8,128)(2,1)} %refs_0_.1) | copy-start | bytes 1572868
  2.3 7.2 %collective-permute-start = (bf16[96,2048]{1,0:T(8,128)(2,1)S(1)}, bf16[96,2048]{1,0:T(8,128)(2,1)S(1)}, u32[]{:S(2)}, u32[]{:S(2)}) collective-permute-start(bf16[96,2048]{1,0:T(8,128)(2,1)S(1)} %get-tuple-element.43), channel_id=1, source_target_pairs={{0,8},{8,0},{16,24},{24,16},{32,40},{40,32},{48,56},{56,48},{64,72... | collective-permute-start | bytes 1179656 | tf_op jit(solution)/shard_map/ppermute | solution.py:54
  5.7 14.7 %collective-permute-start.3 = (bf16[64,4096]{1,0:T(8,128)(2,1)S(1)}, bf16[64,4096]{1,0:T(8,128)(2,1)S(1)}, u32[]{:S(2)}, u32[]{:S(2)}) collective-permute-start(bf16[64,4096]{1,0:T(8,128)(2,1)S(1)} %copy-done.1), channel_id=1, source_target_pairs={{0,1},{1,2},{2,3},{3,0},{4,5},{5,6},{6,7},{7,4},{8,9},{9,10},{10,1... | collective-permute-start | bytes 1572872 | tf_op jit(solution)/shard_map/ppermute | solution.py:45
  5.7 14.7 %collective-permute-start.4 = (bf16[64,4096]{1,0:T(8,128)(2,1)S(1)}, bf16[64,4096]{1,0:T(8,128)(2,1)S(1)}, u32[]{:S(2)}, u32[]{:S(2)}) collective-permute-start(bf16[64,4096]{1,0:T(8,128)(2,1)S(1)} %copy-done.1), channel_id=1, source_target_pairs={{0,3},{1,0},{2,1},{3,2},{4,7},{5,4},{6,5},{7,6},{8,11},{9,8},{10,9... | collective-permute-start | bytes 1572872 | tf_op jit(solution)/shard_map/ppermute | solution.py:45
  8.4 10.2 %collective-permute-start.2 = (bf16[64,2560]{1,0:T(8,128)(2,1)S(1)}, bf16[64,2560]{1,0:T(8,128)(2,1)S(1)}, u32[]{:S(2)}, u32[]{:S(2)}) collective-permute-start(bf16[64,2560]{1,0:T(8,128)(2,1)S(1)} %slice.3), channel_id=1, source_target_pairs={{0,4},{1,5},{2,6},{3,7},{4,0},{5,1},{6,2},{7,3},{8,12},{9,13},{10,... | collective-permute-start | bytes 983048 | tf_op jit(solution)/shard_map/ppermute | solution.py:50
  9.7 11.5 %collective-permute-start.1 = (bf16[96,1024]{1,0:T(8,128)(2,1)S(1)}, bf16[96,1024]{1,0:T(8,128)(2,1)S(1)}, u32[]{:S(2)}, u32[]{:S(2)}) collective-permute-start(bf16[96,1024]{1,0:T(8,128)(2,1)S(1)} %get-tuple-element.44.refs_2_), channel_id=1, source_target_pairs={{0,16},{8,24},{16,0},{24,8},{32,48},{40,56},{48,32},{56,40},{64,80... | collective-permute-start | bytes 589832 | tf_op jit(solution)/shard_map/ppermute | solution.py:54
  10.1 2.2 %copy-start = (bf16[1,512,4096]{2,1,0:T(8,128)(2,1)S(1)}, bf16[1,512,4096]{2,1,0:T(8,128)(2,1)}, u32[]{:S(2)}) copy-start(bf16[1,512,4096]{2,1,0:T(8,128)(2,1)} %param.8) | copy-start | bytes 12582916
  15.6 8.5 %copy-start.7 = (f32[96,128]{1,0:T(8,128)S(1)}, f32[96,128]{1,0:T(8,128)}, u32[]{:S(2)}) copy-start(f32[96,128]{1,0:T(8,128)} %refs_3_.3) | copy-start | bytes 147460
  15.6 8.5 %copy-start.8 = (f32[96,128]{1,0:T(8,128)S(1)}, f32[96,128]{1,0:T(8,128)}, u32[]{:S(2)}) copy-start(f32[96,128]{1,0:T(8,128)} %refs_4_.1) | copy-start | bytes 147460
  15.6 24.0 %collective-permute-start.7 = (bf16[256,1536]{1,0:T(8,128)(2,1)S(1)}, bf16[256,1536]{1,0:T(8,128)(2,1)S(1)}, u32[]{:S(2)}, u32[]{:S(2)}) collective-permute-start(bf16[256,1536]{1,0:T(8,128)(2,1)S(1)} %get-tuple-element.50.refs_5_), channel_id=1, source_target_pairs={{0,4},{1,5},{2,6},{3,7},{4,0},{5,1},{6,2},{7,3},{8,12},{9,13},{10,... | collective-permute-start | bytes 2359304 | tf_op jit(solution)/shard_map/ppermute | solution.py:50
  21.3 18.3 %collective-permute-start.5 = (bf16[64,5888]{1,0:T(8,128)(2,1)S(1)}, bf16[64,5888]{1,0:T(8,128)(2,1)S(1)}, u32[]{:S(2)}, u32[]{:S(2)}) collective-permute-start(bf16[64,5888]{1,0:T(8,128)(2,1)S(1)} %get-tuple-element.51.refs_4_), channel_id=1, source_target_pairs={{0,1},{1,2},{2,3},{3,0},{4,5},{5,6},{6,7},{7,4},{8,9},{9,10},{10,1... | collective-permute-start | bytes 2261000 | tf_op jit(solution)/shard_map/ppermute | solution.py:45
  21.4 18.2 %collective-permute-start.6 = (bf16[64,5888]{1,0:T(8,128)(2,1)S(1)}, bf16[64,5888]{1,0:T(8,128)(2,1)S(1)}, u32[]{:S(2)}, u32[]{:S(2)}) collective-permute-start(bf16[64,5888]{1,0:T(8,128)(2,1)S(1)} %get-tuple-element.56), channel_id=1, source_target_pairs={{0,3},{1,0},{2,1},{3,2},{4,7},{5,4},{6,5},{7,6},{8,11},{9,8},{10,9... | collective-permute-start | bytes 2261000 | tf_op jit(solution)/shard_map/ppermute | solution.py:45
  24.2 10.4 %collective-permute-start.8 = (bf16[96,1152]{1,0:T(8,128)(2,1)S(1)}, bf16[96,1152]{1,0:T(8,128)(2,1)S(1)}, u32[]{:S(2)}, u32[]{:S(2)}) collective-permute-start(bf16[96,1152]{1,0:T(8,128)(2,1)S(1)} %get-tuple-element.52.refs_2_.refs_1_), channel_id=1, source_target_pairs={{0,128},{8,136},{16,144},{24,152},{32,160},{40,168},{48,176},{56,1... | collective-permute-start | bytes 663560 | tf_op jit(solution)/shard_map/ppermute | solution.py:54
  40.0 26.7 %collective-permute-start.10 = (bf16[64,8448]{1,0:T(8,128)(2,1)S(1)}, bf16[64,8448]{1,0:T(8,128)(2,1)S(1)}, u32[]{:S(2)}, u32[]{:S(2)}) collective-permute-start(bf16[64,8448]{1,0:T(8,128)(2,1)S(1)} %get-tuple-element.61), channel_id=1, source_target_pairs={{0,3},{1,0},{2,1},{3,2},{4,7},{5,4},{6,5},{7,6},{8,11},{9,8},{10,9... | collective-permute-start | bytes 3244040 | tf_op jit(solution)/shard_map/ppermute | solution.py:45
  41.3 25.4 %collective-permute-start.9 = (bf16[64,8448]{1,0:T(8,128)(2,1)S(1)}, bf16[64,8448]{1,0:T(8,128)(2,1)S(1)}, u32[]{:S(2)}, u32[]{:S(2)}) collective-permute-start(bf16[64,8448]{1,0:T(8,128)(2,1)S(1)} %get-tuple-element.60), channel_id=1, source_target_pairs={{0,1},{1,2},{2,3},{3,0},{4,5},{5,6},{6,7},{7,4},{8,9},{9,10},{10,1... | collective-permute-start | bytes 3244040 | tf_op jit(solution)/shard_map/ppermute | solution.py:45
  41.6 12.9 %collective-permute-start.11 = (bf16[96,1280]{1,0:T(8,128)(2,1)S(1)}, bf16[96,1280]{1,0:T(8,128)(2,1)S(1)}, u32[]{:S(2)}, u32[]{:S(2)}) collective-permute-start(bf16[96,1280]{1,0:T(8,128)(2,1)S(1)} %get-tuple-element.59.refs_9_.refs_1_), channel_id=1, source_target_pairs={{0,64},{8,72},{16,80},{24,88},{32,96},{40,104},{48,112},{56,120},{... | collective-permute-start | bytes 737288 | tf_op jit(solution)/shard_map/ppermute | solution.py:54
  44.3 28.6 %collective-permute-start.19 = (bf16[256,1536]{1,0:T(8,128)(2,1)S(1)}, bf16[256,1536]{1,0:T(8,128)(2,1)S(1)}, u32[]{:S(2)}, u32[]{:S(2)}) collective-permute-start(bf16[256,1536]{1,0:T(8,128)(2,1)S(1)} %get-tuple-element.66.refs_3_.refs_10_), channel_id=1, source_target_pairs={{0,4},{1,5},{2,6},{3,7},{4,0},{5,1},{6,2},{7,3},{8,12},{9,13},{10,... | collective-permute-start | bytes 2359304 | tf_op jit(solution)/shard_map/ppermute | solution.py:50
  54.5 6.6 %collective-permute-start.12 = (bf16[96,1536]{1,0:T(8,128)(2,1)S(1)}, bf16[96,1536]{1,0:T(8,128)(2,1)S(1)}, u32[]{:S(2)}, u32[]{:S(2)}) collective-permute-start(bf16[96,1536]{1,0:T(8,128)(2,1)S(1)} %get-tuple-element.68.refs_1_), channel_id=1, source_target_pairs={{0,32},{8,40},{16,48},{24,56},{32,0},{40,8},{48,16},{56,24},{64,96... | collective-permute-start | bytes 884744 | tf_op jit(solution)/shard_map/ppermute | solution.py:54
  61.9 4.8 %collective-permute-start.13 = (bf16[96,1024]{1,0:T(8,128)(2,1)S(1)}, bf16[96,1024]{1,0:T(8,128)(2,1)S(1)}, u32[]{:S(2)}, u32[]{:S(2)}) collective-permute-start(bf16[96,1024]{1,0:T(8,128)(2,1)S(1)} %get-tuple-element.69.refs_1_), channel_id=1, source_target_pairs={{0,16},{8,24},{16,0},{24,8},{32,48},{40,56},{48,32},{56,40},{64,80... | collective-permute-start | bytes 589832 | tf_op jit(solution)/shard_map/ppermute | solution.py:54
  66.9 16.9 %collective-permute-start.14 = (bf16[64,2560]{1,0:T(8,128)(2,1)S(1)}, bf16[64,2560]{1,0:T(8,128)(2,1)S(1)}, u32[]{:S(2)}, u32[]{:S(2)}) collective-permute-start(bf16[64,2560]{1,0:T(8,128)(2,1)S(1)} %get-tuple-element.70), channel_id=1, source_target_pairs={{0,4},{1,5},{2,6},{3,7},{4,0},{5,1},{6,2},{7,3},{8,12},{9,13},{10,... | collective-permute-start | bytes 983048 | tf_op jit(solution)/shard_map/ppermute | solution.py:50
  69.5 11.9 %collective-permute-start.17 = (bf16[96,1024]{1,0:T(8,128)(2,1)S(1)}, bf16[96,1024]{1,0:T(8,128)(2,1)S(1)}, u32[]{:S(2)}, u32[]{:S(2)}) collective-permute-start(bf16[96,1024]{1,0:T(8,128)(2,1)S(1)} %get-tuple-element.69.refs_1_), channel_id=1, source_target_pairs={{0,8},{8,0},{16,24},{24,16},{32,40},{40,32},{48,56},{56,48},{64,72... | collective-permute-start | bytes 589832 | tf_op jit(solution)/shard_map/ppermute | solution.py:54
  72.8 8.6 %collective-permute-start.18 = (bf16[96,1024]{1,0:T(8,128)(2,1)S(1)}, bf16[96,1024]{1,0:T(8,128)(2,1)S(1)}, u32[]{:S(2)}, u32[]{:S(2)}) collective-permute-start(bf16[96,1024]{1,0:T(8,128)(2,1)S(1)} %shard_map.128.refs_5_.refs_3_), channel_id=1, source_target_pairs={{0,8},{8,0},{16,24},{24,16},{32,40},{40,32},{48,56},{56,48},{64,72... | collective-permute-start | bytes 589832 | tf_op jit(solution)/shard_map/ppermute | solution.py:54
  72.8 11.0 %collective-permute-start.15 = (bf16[64,1536]{1,0:T(8,128)(2,1)S(1)}, bf16[64,1536]{1,0:T(8,128)(2,1)S(1)}, u32[]{:S(2)}, u32[]{:S(2)}) collective-permute-start(bf16[64,1536]{1,0:T(8,128)(2,1)S(1)} %get-tuple-element.72.refs_12_), channel_id=1, source_target_pairs={{0,1},{1,2},{2,3},{3,0},{4,5},{5,6},{6,7},{7,4},{8,9},{9,10},{10,1... | collective-permute-start | bytes 589832 | tf_op jit(solution)/shard_map/ppermute | solution.py:45
  72.9 8.5 %copy-start.4 = (bf16[1,96,4096]{2,1,0:T(8,128)(2,1)S(1)}, bf16[1,96,4096]{2,1,0:T(8,128)(2,1)}, u32[]{:S(2)}) copy-start(bf16[1,96,4096]{2,1,0:T(8,128)(2,1)} %param.11) | copy-start | bytes 2359300
  72.9 10.9 %collective-permute-start.16 = (bf16[64,1536]{1,0:T(8,128)(2,1)S(1)}, bf16[64,1536]{1,0:T(8,128)(2,1)S(1)}, u32[]{:S(2)}, u32[]{:S(2)}) collective-permute-start(bf16[64,1536]{1,0:T(8,128)(2,1)S(1)} %get-tuple-element.73), channel_id=1, source_target_pairs={{0,3},{1,0},{2,1},{3,2},{4,7},{5,4},{6,5},{7,6},{8,11},{9,8},{10,9... | collective-permute-start | bytes 589832 | tf_op jit(solution)/shard_map/ppermute | solution.py:45
  81.4 1.0 %copy-start.6 = (bf16[512,512]{1,0:T(8,128)(2,1)S(1)}, bf16[512,512]{1,0:T(8,128)(2,1)}, u32[]{:S(2)}) copy-start(bf16[512,512]{1,0:T(8,128)(2,1)} %get-tuple-element.37.refs_5_) | copy-start | bytes 1572868
  83.8 1.1 %copy-start.2 = (bf16[96,4096]{1,0:T(8,128)(2,1)S(1)}, bf16[96,4096]{1,0:T(8,128)(2,1)}, u32[]{:S(2)}) copy-start(bf16[96,4096]{1,0:T(8,128)(2,1)} %shard_map.131.refs_7_) | copy-start | bytes 2359300

commit v3 on v2

--- a/solution.py
+++ b/solution.py
@@ -15,13 +15,12 @@
 LANE = 128
 ORDER = (0, 3, 1, 2)
 Y_LEFT, Y_RIGHT = slice(2560, 3328), slice(3328, 4096)
-VMEM_LIMIT = 24 * 1024 * 1024
-
-
-def call(kernel, outs, *args, deps=(), cost=None, **kw):
-    if cost is None:
-        size = sum(a.size * a.dtype.itemsize for a in (*args, *jax.tree.leaves(outs)))
-        cost = pl.CostEstimate(flops=0, bytes_accessed=size, transcendentals=0)
+EARLY_COST = pl.CostEstimate(flops=0, bytes_accessed=64 << 20, transcendentals=0)
+COST = pl.CostEstimate(flops=1, bytes_accessed=1024, transcendentals=0)
+VMEM_LIMIT = 20 * 1024 * 1024
+
+
+def call(kernel, outs, *args, deps=(), cost=COST, **kw):
     if "in_specs" not in kw:
         vmem = pl.BlockSpec(memory_space=pltpu.VMEM)
         kw.update(in_specs=[vmem] * len(args), out_specs=jax.tree.map(lambda _: vmem, outs))
@@ -75,40 +74,16 @@
     return jnp.dot(x, y, preferred_element_type=F32).astype(BF)
 
 
-def early_kernel(a_hbm, w_hbm, rel, w, p2a, p2b, py1, a, sems):
+def early_kernel(a, w, rel, p2a, p2b, py1):
     d = w.shape[1]
-    order = blocks(CX, d) + blocks(0, CX)
-    copies = [pltpu.make_async_copy(a_hbm, a, sems.at[len(order)])]
-    for i, k in enumerate(order):
-        at = pl.ds(k.start, CB)
-        copies.append(pltpu.make_async_copy(w_hbm.at[:, at], w.at[:, at], sems.at[i]))
-    for copy in copies:
-        copy.start()
-    copies[0].wait()
     arrange_rows(a, rel)
     turned = jnp.concatenate([rel[yi * 128 + 64 : yi * 128 + 128, :] for yi in range(NY)], 0)
-    for copy, k in zip(copies[1:], order):
-        copy.wait()
-        if k.start >= CX:
-            py1[:, k.start - CX : k.stop - CX] = dot(turned, w[:, k])
-        else:
-            p = dot(rel[384:512, :], w[:, k])
-            p2a[:, k] = p[0:64]
-            p2b[:, k] = p[64:128]
-
-
-def early(a, w, deps):
-    d = w.shape[1]
-    hbm, vmem = pl.BlockSpec(memory_space=pl.ANY), pl.BlockSpec(memory_space=pltpu.VMEM)
-    return call(
-        early_kernel,
-        [sds(512, 512), sds(512, d), sds(64, CX), sds(64, CX), sds(256, d - CX)],
-        a, w, deps=deps,
-        in_specs=[hbm, hbm],
-        out_specs=[vmem] * 5,
-        scratch_shapes=[pltpu.VMEM((512, 512), BF), pltpu.SemaphoreType.DMA((d // CB + 1,))],
-        cost=pl.CostEstimate(flops=0, bytes_accessed=12 << 20, transcendentals=0),
-    )
+    for k in blocks(CX, d):
+        py1[:, k.start - CX : k.stop - CX] = dot(turned, w[:, k])
+    for k in blocks(0, CX):
+        p = dot(rel[384:512, :], w[:, k])
+        p2a[:, k] = p[0:64]
+        p2b[:, k] = p[64:128]
 
 
 def late_kernel(rel, w, p00, p01, pm, pp, py0):
@@ -124,50 +99,86 @@
         py0[:, k.start - CX : k.stop - CX] = dot(kept, w[:, k])
 
 
-def grads_kernel(rel, w, gg, x1, ym, mu, yp, md, fu, fd, y4, yx, wg_hbm, hg, wg, g, sems):
-    d = w.shape[1]
+def dot_nt(x, y):
+    return lax.dot_general(x, y, (((1,), (1,)), ((), ())), preferred_element_type=F32)
+
+
+def grads_x_kernel(rel, w, gg, x1, ym, mu, yp, md, part_wg, part_hg, g):
+    for n, (r, first) in enumerate(((gg, 0), (x1, 0), (ym, 0), (mu, CX), (yp, 0), (md, CX))):
+        g[n * 64 : n * 64 + 64, :] = r[:, first : first + CX]
+    across = rel[0:384, :].T
+    for k in blocks(0, CX):
+        part_wg[:, k] = jnp.dot(across, g[:, k], preferred_element_type=F32)
+    part_hg[...] = dot_nt(g[...], w[:, 0:CX])
+
+
+def grads_y_kernel(rel, w, y4, yx, wg_hbm, part_hg, wg, g, sems):
     across = rel[...].T
     copies = []
-    for i, k in enumerate(blocks(0, d)):
-        if k.start < CX:
-            near, far = (slice(n * CX + k.start, n * CX + k.stop) for n in (1, 2))
-            parts = (gg[:, k], x1[:, k], ym[:, k], mu[:, near], yp[:, k], md[:, near], fu[:, far], fd[:, far])
-        else:
-            cols = slice(k.start - CX, k.stop - CX)
-            parts = [r[yi * 64 : yi * 64 + 64, cols] for yi in range(NY) for r in (y4, yx)]
-        for n, p in enumerate(parts):
-            g[n * 64 : n * 64 + 64, k] = p
+    for i, k in enumerate(blocks(0, y4.shape[1])):
+        for n in range(NY):
+            g[n * 128 : n * 128 + 64, k] = y4[n * 64 : n * 64 + 64, k]
+            g[n * 128 + 64 : n * 128 + 128, k] = yx[n * 64 : n * 64 + 64, k]
         wg[:, k] = dot(across, g[:, k])
+        copies.append(
+            pltpu.make_async_copy(
+                wg.at[:, pl.ds(k.start, CB)], wg_hbm.at[:, pl.ds(CX + k.start, CB)], sems.at[i]
+            )
+        )
+        copies[-1].start()
+    part_hg[...] = dot_nt(g[...], w[:, CX:])
+    for copy in copies:
+        copy.wait()
+
+
+def grads_y(rel, w, y4, yx, deps):
+    d, cy = w.shape[1], y4.shape[1]
+    hbm, vmem = pl.BlockSpec(memory_space=pltpu.HBM), pl.BlockSpec(memory_space=pltpu.VMEM)
+    return call(
+        grads_y_kernel, [sds(512, d), sds(512, 512, dtype=F32)], rel, w, y4, yx, deps=deps,
+        in_specs=[vmem] * 4,
+        out_specs=[hbm, vmem],
+        scratch_shapes=[
+            pltpu.VMEM((512, cy), BF),
+            pltpu.VMEM((512, cy), BF),
+            pltpu.SemaphoreType.DMA((len(blocks(0, cy)),)),
+        ],
+    )
+
+
+def last_grads_kernel(old, rel, w, fu, fd, part_wg, hx, hy, wg_hbm, hg, done, wg, sems):
+    across = rel[384:512, :].T
+    done[...] = jnp.zeros_like(done)
+    last = jnp.concatenate([r[:, 2 * CX : 3 * CX] for r in (fu, fd)], 0)
+    copies = []
+    for i, k in enumerate(blocks(0, CX)):
+        more = jnp.dot(across, last[:, k], preferred_element_type=F32)
+        wg[:, k] = (part_wg[:, k] + more).astype(BF)
         at = pl.ds(k.start, CB)
         copies.append(pltpu.make_async_copy(wg.at[:, at], wg_hbm.at[:, at], sems.at[i]))
         copies[-1].start()
-    h = lax.dot_general(
-        g[...], w[...], (((1,), (1,)), ((), ())), preferred_element_type=F32
-    ).astype(BF)
+    more = dot_nt(last, w[:, 0:CX])
     for yi in range(NY):
         for xi in range(NX):
-            at = pl.multiple_of(row_block(yi, xi) * 64, 64)
+            at = pl.ds(pl.multiple_of(row_block(yi, xi) * 64, 64), 64)
             n = (yi * NX + xi) * 64
-            hg[pl.ds(at, 64), :] = h[n : n + 64]
+            rows = hx[n : n + 64, :] if yi < 3 else more[xi * 64 : xi * 64 + 64]
+            hg[at, :] = (hy[n : n + 64, :] + rows).astype(BF)
     for copy in copies:
         copy.wait()
 
 
-def grads(rel, w, *parts, deps):
+def last_grads(old, rel, w, fu, fd, part_wg, hx, hy, deps):
     d = w.shape[1]
-    hbm, vmem = pl.BlockSpec(memory_space=pl.ANY), pl.BlockSpec(memory_space=pltpu.VMEM)
+    hbm, vmem = pl.BlockSpec(memory_space=pltpu.HBM), pl.BlockSpec(memory_space=pltpu.VMEM)
     return call(
-        grads_kernel,
-        [sds(512, d), sds(512, 512)],
-        rel, w, *parts, deps=deps,
-        in_specs=[vmem] * (2 + len(parts)),
-        out_specs=[hbm, vmem],
-        scratch_shapes=[
-            pltpu.VMEM((512, d), BF),
-            pltpu.VMEM((512, d), BF),
-            pltpu.SemaphoreType.DMA((d // CB,)),
-        ],
-        cost=pl.CostEstimate(flops=0, bytes_accessed=16 << 20, transcendentals=0),
+        last_grads_kernel,
+        [sds(512, d), sds(512, 512), sds(8, LANE, dtype=F32)],
+        old, rel, w, fu, fd, part_wg, hx, hy, deps=deps,
+        in_specs=[hbm] + [vmem] * 7,
+        out_specs=[hbm, vmem, vmem],
+        input_output_aliases={0: 0},
+        scratch_shapes=[pltpu.VMEM((512, CX), BF), pltpu.SemaphoreType.DMA((len(blocks(0, CX)),))],
     )
 
 
@@ -186,7 +197,8 @@
         send[:, lanes(i)] = d_ref[:, lanes(2 * i + 1 - c)].astype(BF)
 
 
-def round2_kernel(p2a, p2b, x1, ym, yp, up, down):
+def round2_kernel(p2a, p2b, x1, ym, yp, py1, up, down, turn):
+    turn[...] = py1[...]
     for out, p, y, cols in ((up, p2a, ym, Y_LEFT), (down, p2b, yp, Y_RIGHT)):
         out[:, 0:CX] = p[...]
         out[:, CX : 2 * CX] = x1[...]
@@ -218,19 +230,23 @@
 
 
 def round4_kernel(p01, fu, fd, qp, qm, up, down, x):
-    half = qp.shape[1] // 2
+    cy = qp.shape[1]
+    half = cy // 2
     x[...] = (f32(p01) + f32(fu.at[:, CX : 2 * CX]) + f32(fd.at[:, CX : 2 * CX])).astype(BF)
     up[:, 0:half] = (qp[:, 0:half] + f32(fu.at[:, 3 * CX :])).astype(BF)
-    up[:, half:] = qp[:, half:].astype(BF)
+    up[:, half:cy] = qp[:, half:].astype(BF)
     down[:, 0:half] = qm[:, 0:half].astype(BF)
-    down[:, half:] = (qm[:, half:] + f32(fd.at[:, 3 * CX :])).astype(BF)
+    down[:, half:cy] = (qm[:, half:] + f32(fd.at[:, 3 * CX :])).astype(BF)
+    up[:, cy:] = jnp.zeros((64, LANE), BF)
+    down[:, cy:] = jnp.zeros((64, LANE), BF)
 
 
 def finish_kernel(p00, sp, sm, x, q0, s1, s2, o):
     o[:, 0:CX] = (
         f32(p00) + f32(sp.at[:, 0:CX]) + f32(sm.at[:, 0:CX]) + f32(x)
     ).astype(BF)
-    o[:, CX:] = (f32(q0) + f32(s1) + f32(s2)).astype(BF)
+    cy = q0.shape[1]
+    o[:, CX:] = (f32(q0) + f32(s1.at[:, 0:cy]) + f32(s2.at[:, 0:cy])).astype(BF)
 
 
 def bits():
@@ -320,16 +336,20 @@
     yp = send_y(output_grad, -1)
     keep, send = call(core_split_kernel, [sds(rows, d // 2)] * 2, delta)
     c1 = send_replica(send, 1)
-    keep, send = call(core_add_kernel, [f(rows, n), sds(rows, n)], keep, c1)
+    rel, p2a, p2b, py1 = call(
+        early_kernel, [sds(512, 512), sds(64, CX), sds(64, CX), sds(256, cy)], heads, weight,
+        cost=EARLY_COST,
+    )
+    w = weight
+    keep, send = call(core_add_kernel, [f(rows, n), sds(rows, n)], keep, c1, deps=(py1,))
     xl = send_replica(send, 2)
 
-    rel, w, p2a, p2b, py1 = early(heads, weight, (send,))
+    up, down, py1 = call(
+        round2_kernel, [sds(64, 2 * CX + cy // 2)] * 2 + [sds(256, cy)],
+        p2a, p2b, x1, ym, yp, py1, deps=(xl,),
+    )
+    mu, md = send_y(up, 1), send_y(down, -1)
     yx = send_x(py1)
-
-    up, down = call(
-        round2_kernel, [sds(64, 2 * CX + cy // 2)] * 2, p2a, p2b, x1, ym, yp, deps=(py1, xl)
-    )
-    mu, md = send_y(up, 1), send_y(down, -1)
     keep, mine = call(
         x_add_kernel, [f(rows, n), sds(rows, n + LANE)], keep, xl, global_slice, momentum, deps=(up,)
     )
@@ -338,7 +358,6 @@
         late_kernel,
         [sds(64, CX), sds(64, CX), sds(128, CX), sds(128, CX), sds(256, cy)],
         rel, w, deps=(mine,),
-        cost=pl.CostEstimate(flops=0, bytes_accessed=8 << 20, transcendentals=0),
     )
     keep, mine = call(
         part(z_add_kernel, 4), [f(rows, n), sds(rows, n + 2 * LANE)], keep, mine, z4, deps=(py0,)
@@ -352,8 +371,12 @@
     )
     fu, fd = send_y(up, 1), send_y(down, -1)
     gyx = send_x(y4)
+    part_wg, part_hx = call(
+        grads_x_kernel, [f(512, CX), f(384, 512)], rel, w, output_grad, x1, ym, mu, yp, md,
+        deps=(y4,), scratch_shapes=[pltpu.VMEM((384, CX), BF)],
+    )
     keep, mine = call(
-        part(z_add_kernel, 2), [f(rows, n), sds(rows, n + 4 * LANE)], keep, mine, z2, deps=(y4,)
+        part(z_add_kernel, 2), [f(rows, n), sds(rows, n + 4 * LANE)], keep, mine, z2, deps=(part_hx,)
     )
     z1 = send_replica(mine, 4)
     q00, new_global, new_momentum = call(
@@ -361,19 +384,21 @@
         keep, mine, z1, global_slice, momentum,
     )
     q01 = send_replica(q00, 1)
-    q10 = call(copy_kernel, sds(rows, n), send_replica(q00, 2))
-    q11 = send_replica(q10, 1)
+    weight_grad, part_hy = grads_y(rel, w, y4, gyx, deps=(q00,))
+    q10 = send_replica(q00, 2)
 
     up, down, x = call(
-        round4_kernel, [sds(64, cy), sds(64, cy), sds(64, CX)], p01, fu, fd, qp, qm, deps=(q10,)
+        round4_kernel, [sds(64, cy + LANE), sds(64, cy + LANE), sds(64, CX)], p01, fu, fd, qp, qm, deps=(part_hy,)
     )
     s1, s2 = send_y(up, 1), send_y(down, -1)
     x = send_x(x)
-    weight_grad, head_grads = grads(
-        rel, w, output_grad, x1, ym, mu, yp, md, fu, fd, y4, gyx, deps=(up,)
-    )
-    merged = call(merge_kernel, sds(rows, d), local, q00, q01, q10, q11, deps=(head_grads,))
-    projected = call(finish_kernel, sds(64, d), p00, fu, fd, x, q0, s1, s2, deps=(merged,))
+    q10 = call(copy_kernel, sds(rows, n), q10, deps=(up,))
+    q11 = send_replica(q10, 1)
+    weight_grad, head_grads, done = last_grads(
+        weight_grad, rel, w, fu, fd, part_wg, part_hx, part_hy, deps=(up,)
+    )
+    merged = call(merge_kernel, sds(rows, d), local, q00, q01, q10, q11, deps=(done,))
+    projected = call(finish_kernel, sds(64, d), p00, fu, fd, x, q0, s1, s2, deps=(done,))
     return (projected, head_grads, weight_grad[None], merged[None], new_global, new_momentum)
 
 

time: 86.2 us -> 84.3 us (0.978)
  local copies, waits for them, and re-layouts: 5.86 us -> 3.7 us
    ppermute x8, waiting for transfers between devices: 1.78 us -> 6.36 us  [send_y(): return lax.ppermute(x, 'tensor', pairs)]
    ppermute x8, waiting for transfers between devices: 21.2 us -> 17.3 us  [send_replica(): lax.ppermute(x, 'replica', [(r, r ^ bit) for r in range(lax.axis_size('re...]
    ppermute x4, starting transfers between devices: 7.33 us -> 4.94 us  [send_x(): return lax.ppermute(x, 'tensor', pairs)]
    unnamed x18 -> x16, local copies, waits for them, and re-layouts: 5.84 us -> 3.68 us
    ppermute x8, starting transfers between devices: 18 us -> 19.9 us  [send_replica(): lax.ppermute(x, 'replica', [(r, r ^ bit) for r in range(lax.axis_size('re...]
    ppermute x8, starting transfers between devices: 9.66 us -> 10.8 us  [send_y(): return lax.ppermute(x, 'tensor', pairs)]
    pallas_call x15 -> x17, Pallas kernels: 15.1 us -> 15 us  [call(): pl.pallas_call(body, out_shape=outs, cost_estimate=cost, compiler_params=...]
  transfers between devices with their start and end apart: 20 -> 20, of which waited for: 8 -> 7; matrix products, arithmetic and copies ran while one was open for 0% -> 0% of each run, Pallas kernels for 16% -> 16%
where the time goes in v3:
time: 84.3 us; the launch traced here: 84.2 us
  starting transfers between devices  35.7 us (42%)
  waiting for transfers between devices  28.9 us (34%)
  Pallas kernels  15 us (18%)
  local copies, waits for them, and re-layouts  3.7 us (4%)
  between operations  0.85 us (1%)
    ppermute x8, starting transfers between devices, send_replica(): lax.ppermute(x, 'replica', [(r, r ^ bit) for r in range(lax.axis_size('re...  19.9 us
    ppermute x8, waiting for transfers between devices, send_replica(): lax.ppermute(x, 'replica', [(r, r ^ bit) for r in range(lax.axis_size('re...  17.3 us
    pallas_call x17, Pallas kernels, call(): pl.pallas_call(body, out_shape=outs, cost_estimate=cost, compiler_params=...  15 us
    ppermute x8, starting transfers between devices, send_y(): return lax.ppermute(x, 'tensor', pairs)  10.8 us
    ppermute x8, waiting for transfers between devices, send_y(): return lax.ppermute(x, 'tensor', pairs)  6.36 us
    ppermute x4, waiting for transfers between devices, send_x(): return lax.ppermute(x, 'tensor', pairs)  5.29 us
    ppermute x4, starting transfers between devices, send_x(): return lax.ppermute(x, 'tensor', pairs)  4.94 us
    unnamed x16, local copies, waits for them, and re-layouts  3.68 us
  transfers between devices with their start and end apart: 20, of which 7 were waited for; matrix products, arithmetic and copies ran while one was open for 0% of the time, Pallas kernels for 16%

profile of v3, /device:TPU:1, one launch (start us, length us, event | category | flops | bytes accessed | tf_op | source)
XLA Modules:
  0.0 84.2 jit_solution(322341499461074969)
XLA Ops:
  0.7 1.5 %copy-done.3 = f32[1,96,4096]{2,1,0:T(8,128)S(1)} copy-done((f32[1,96,4096]{2,1,0:T(8,128)S(1)}, f32[1,96,4096]{2,1,0:T(8,128)}, u32[]{:S(2)}) %copy-start.3) | copy-done | bytes 1572888
  2.1 0.2 shard_map.119
  2.3 3.3 %collective-permute-start = (bf16[96,2048]{1,0:T(8,128)(2,1)S(1)}, bf16[96,2048]{1,0:T(8,128)(2,1)S(1)}, u32[]{:S(2)}, u32[]{:S(2)}) collective-permute-start(bf16[96,2048]{1,0:T(8,128)(2,1)S(1)} %get-tuple-element.49), channel_id=1, source_target_pairs={{0,8},{8,0},{16,24},{24,16},{32,40},{40,32},{48,56},{56,48},{64,72... | collective-permute-start | bytes 1179656 | tf_op jit(solution)/shard_map/ppermute | solution.py:53
  5.7 0.0 copy-done.2
  5.7 0.0 collective-permute-start.3
  5.7 2.7 %collective-permute-start.4 = (bf16[64,4096]{1,0:T(8,128)(2,1)S(1)}, bf16[64,4096]{1,0:T(8,128)(2,1)S(1)}, u32[]{:S(2)}, u32[]{:S(2)}) collective-permute-start(bf16[64,4096]{1,0:T(8,128)(2,1)S(1)} %copy-done.2), channel_id=1, source_target_pairs={{0,3},{1,0},{2,1},{3,2},{4,7},{5,4},{6,5},{7,6},{8,11},{9,8},{10,9... | collective-permute-start | bytes 1572872 | tf_op jit(solution)/shard_map/ppermute | solution.py:44
  8.4 1.1 %collective-permute-start.2 = (bf16[64,2560]{1,0:T(8,128)(2,1)S(1)}, bf16[64,2560]{1,0:T(8,128)(2,1)S(1)}, u32[]{:S(2)}, u32[]{:S(2)}) collective-permute-start(bf16[64,2560]{1,0:T(8,128)(2,1)S(1)} %slice.3), channel_id=1, source_target_pairs={{0,4},{1,5},{2,6},{3,7},{4,0},{5,1},{6,2},{7,3},{8,12},{9,13},{10,... | collective-permute-start | bytes 983048 | tf_op jit(solution)/shard_map/ppermute | solution.py:49
  9.5 0.0 copy-done.5
  9.5 2.2 %copy-done = bf16[1,512,4096]{2,1,0:T(8,128)(2,1)S(1)} copy-done((bf16[1,512,4096]{2,1,0:T(8,128)(2,1)S(1)}, bf16[1,512,4096]{2,1,0:T(8,128)(2,1)}, u32[]{:S(2)}) %copy-start) | copy-done | bytes 4194328
  11.7 0.9 %shard_map.118 = (bf16[512,512]{1,0:T(8,128)(2,1)S(1)}, bf16[64,2560]{1,0:T(8,128)(2,1)S(1)}, bf16[64,2560]{1,0:T(8,128)(2,1)S(1)}, bf16[256,1536]{1,0:T(8,128)(2,1)S(1)}) custom-call(bf16[512,512]{1,0:T(8,128)(2,1)S(1)} %copy-done.5, bf16[512,4096]{1,0:T(8,128)(2,1)S(1)} %bitcast.5), custom_call_target="tpu_custom_call" | custom-call | bytes 67108864 | tf_op jit(solution)/shard_map/pallas_call | solution.py:32
  12.6 0.0 collective-permute-done.refs_1_
  12.6 0.2 shard_map.120
  12.9 0.0 copy-start.6
  12.9 0.0 copy-start.7
  12.9 0.4 collective-permute-start.1
  13.3 5.3 %collective-permute-done.2.refs_2_.refs_3_ = bf16[64,2560]{1,0:T(8,128)(2,1)S(1)} collective-permute-done((bf16[64,2560]{1,0:T(8,128)(2,1)S(1)}, bf16[64,2560]{1,0:T(8,128)(2,1)S(1)}, u32[]{:S(2)}, u32[]{:S(2)}) %collective-permute-start.2) | collective-permute-done | bytes 327712 | tf_op jit(solution)/shard_map/ppermute | solution.py:49
  18.6 1.8 %collective-permute-done.3.refs_3_.refs_4_ = bf16[64,4096]{1,0:T(8,128)(2,1)S(1)} collective-permute-done((bf16[64,4096]{1,0:T(8,128)(2,1)S(1)}, bf16[64,4096]{1,0:T(8,128)(2,1)S(1)}, u32[]{:S(2)}, u32[]{:S(2)}) %collective-permute-start.3) | collective-permute-done | bytes 524320 | tf_op jit(solution)/shard_map/ppermute | solution.py:44
  20.3 0.0 collective-permute-done.4.refs_4_.refs_6_
  20.4 0.9 %collective-permute-done.1.refs_6_.refs_1_ = bf16[96,1024]{1,0:T(8,128)(2,1)S(1)} collective-permute-done((bf16[96,1024]{1,0:T(8,128)(2,1)S(1)}, bf16[96,1024]{1,0:T(8,128)(2,1)S(1)}, u32[]{:S(2)}, u32[]{:S(2)}) %collective-permute-start.1) | collective-permute-done | bytes 196640 | tf_op jit(solution)/shard_map/ppermute | solution.py:53
  21.2 0.1 shard_map.121
  21.4 1.8 %collective-permute-start.7 = (bf16[256,1536]{1,0:T(8,128)(2,1)S(1)}, bf16[256,1536]{1,0:T(8,128)(2,1)S(1)}, u32[]{:S(2)}, u32[]{:S(2)}) collective-permute-start(bf16[256,1536]{1,0:T(8,128)(2,1)S(1)} %get-tuple-element.62), channel_id=1, source_target_pairs={{0,4},{1,5},{2,6},{3,7},{4,0},{5,1},{6,2},{7,3},{8,12},{9,13},{10,... | collective-permute-start | bytes 2359304 | tf_op jit(solution)/shard_map/ppermute | solution.py:49
  23.2 0.0 collective-permute-start.5
  23.2 2.7 %collective-permute-start.6 = (bf16[64,5888]{1,0:T(8,128)(2,1)S(1)}, bf16[64,5888]{1,0:T(8,128)(2,1)S(1)}, u32[]{:S(2)}, u32[]{:S(2)}) collective-permute-start(bf16[64,5888]{1,0:T(8,128)(2,1)S(1)} %get-tuple-element.60), channel_id=1, source_target_pairs={{0,3},{1,0},{2,1},{3,2},{4,7},{5,4},{6,5},{7,6},{8,11},{9,8},{10,9... | collective-permute-start | bytes 2261000 | tf_op jit(solution)/shard_map/ppermute | solution.py:44
  25.9 0.0 copy-done.7
  25.9 0.1 shard_map.122
  26.0 7.0 %collective-permute-start.8 = (bf16[96,1152]{1,0:T(8,128)(2,1)S(1)}, bf16[96,1152]{1,0:T(8,128)(2,1)S(1)}, u32[]{:S(2)}, u32[]{:S(2)}) collective-permute-start(bf16[96,1152]{1,0:T(8,128)(2,1)S(1)} %get-tuple-element.56.refs_2_.refs_1_), channel_id=1, source_target_pairs={{0,128},{8,136},{16,144},{24,152},{32,160},{40,168},{48,176},{56,1... | collective-permute-start | bytes 663560 | tf_op jit(solution)/shard_map/ppermute | solution.py:53
  33.0 1.6 %shard_map.123 = (bf16[64,2560]{1,0:T(8,128)(2,1)S(1)}, bf16[64,2560]{1,0:T(8,128)(2,1)S(1)}, bf16[128,2560]{1,0:T(8,128)(2,1)S(1)}, bf16[128,2560]{1,0:T(8,128)(2,1)S(1)}, bf16[256,1536]{1,0:T(8,128)(2,1)S(1)}) custom-call(bf16[512,512]{1,0:T(8,128)(2,1)S(1)} %get-tuple-element.47.refs_0_.refs_1_, bf16[512,4096]{1,0:T(8,128)(2,1)S(1)} %bitcast.6, ...), custom_call_target="tpu_custom_call" | custom-call | flops 1 | bytes 1024 | tf_op jit(solution)/shard_map/pallas_call | solution.py:32
  34.6 1.8 %collective-permute-done.8.refs_2_ = bf16[96,1152]{1,0:T(8,128)(2,1)S(1)} collective-permute-done((bf16[96,1152]{1,0:T(8,128)(2,1)S(1)}, bf16[96,1152]{1,0:T(8,128)(2,1)S(1)}, u32[]{:S(2)}, u32[]{:S(2)}) %collective-permute-start.8) | collective-permute-done | bytes 221216 | tf_op jit(solution)/shard_map/ppermute | solution.py:53
  36.4 0.1 shard_map.124
  36.4 4.6 %collective-permute-done.5.refs_2_.refs_5_ = bf16[64,5888]{1,0:T(8,128)(2,1)S(1)} collective-permute-done((bf16[64,5888]{1,0:T(8,128)(2,1)S(1)}, bf16[64,5888]{1,0:T(8,128)(2,1)S(1)}, u32[]{:S(2)}, u32[]{:S(2)}) %collective-permute-start.5) | collective-permute-done | bytes 753696 | tf_op jit(solution)/shard_map/ppermute | solution.py:44
  41.0 0.0 collective-permute-done.6.refs_3_.refs_7_
  41.0 0.0 collective-permute-done.7.refs_8_
  41.0 0.4 shard_map.125
  41.4 0.1 collective-permute-start.9
  41.5 2.7 %collective-permute-start.10 = (bf16[64,8448]{1,0:T(8,128)(2,1)S(1)}, bf16[64,8448]{1,0:T(8,128)(2,1)S(1)}, u32[]{:S(2)}, u32[]{:S(2)}) collective-permute-start(bf16[64,8448]{1,0:T(8,128)(2,1)S(1)} %get-tuple-element.66), channel_id=1, source_target_pairs={{0,3},{1,0},{2,1},{3,2},{4,7},{5,4},{6,5},{7,6},{8,11},{9,8},{10,9... | collective-permute-start | bytes 3244040 | tf_op jit(solution)/shard_map/ppermute | solution.py:44
  44.2 1.3 %collective-permute-start.11 = (bf16[256,1536]{1,0:T(8,128)(2,1)S(1)}, bf16[256,1536]{1,0:T(8,128)(2,1)S(1)}, u32[]{:S(2)}, u32[]{:S(2)}) collective-permute-start(bf16[256,1536]{1,0:T(8,128)(2,1)S(1)} %get-tuple-element.70.refs_8_.refs_2_), channel_id=1, source_target_pairs={{0,4},{1,5},{2,6},{3,7},{4,0},{5,1},{6,2},{7,3},{8,12},{9,13},{10,... | collective-permute-start | bytes 2359304 | tf_op jit(solution)/shard_map/ppermute | solution.py:49
  45.4 3.4 %collective-permute-start.12 = (bf16[96,1280]{1,0:T(8,128)(2,1)S(1)}, bf16[96,1280]{1,0:T(8,128)(2,1)S(1)}, u32[]{:S(2)}, u32[]{:S(2)}) collective-permute-start(bf16[96,1280]{1,0:T(8,128)(2,1)S(1)} %get-tuple-element.64.refs_9_.refs_1_), channel_id=1, source_target_pairs={{0,64},{8,72},{16,80},{24,88},{32,96},{40,104},{48,112},{56,120},{... | collective-permute-start | bytes 737288 | tf_op jit(solution)/shard_map/ppermute | solution.py:53
  48.8 2.6 %shard_map.126 = (f32[512,2560]{1,0:T(8,128)S(1)}, f32[384,512]{1,0:T(8,128)S(1)}) custom-call(bf16[512,512]{1,0:T(8,128)(2,1)S(1)} %get-tuple-element.47.refs_0_.refs_1_, bf16[512,4096]{1,0:T(8,128)(2,1)S(1)} %bitcast.7, bf16[64,4096]{1,0:T(8,128)(2,1)S(1)} %copy-done.2, bf16[64,2560]{1,0:T(8,128)(2,1)S(1)} %collective-permute-done.2.refs_2_.refs_3_, ...), custom_call_target="tpu_custom_call" | custom-call | flops 1 | bytes 1024 | tf_op jit(solution)/shard_map/pallas_call | solution.py:32
  51.4 8.1 %collective-permute-done.12.refs_2_ = bf16[96,1280]{1,0:T(8,128)(2,1)S(1)} collective-permute-done((bf16[96,1280]{1,0:T(8,128)(2,1)S(1)}, bf16[96,1280]{1,0:T(8,128)(2,1)S(1)}, u32[]{:S(2)}, u32[]{:S(2)}) %collective-permute-start.12) | collective-permute-done | bytes 245792 | tf_op jit(solution)/shard_map/ppermute | solution.py:53
  59.4 0.1 shard_map.127
  59.5 0.6 collective-permute-start.13
  60.1 6.5 %collective-permute-done.13.refs_2_ = bf16[96,1536]{1,0:T(8,128)(2,1)S(1)} collective-permute-done((bf16[96,1536]{1,0:T(8,128)(2,1)S(1)}, bf16[96,1536]{1,0:T(8,128)(2,1)S(1)}, u32[]{:S(2)}, u32[]{:S(2)}) %collective-permute-start.13) | collective-permute-done | bytes 294944 | tf_op jit(solution)/shard_map/ppermute | solution.py:53
  66.6 0.7 shard_map.128
  67.3 1.2 %collective-permute-start.18 = (bf16[96,1024]{1,0:T(8,128)(2,1)S(1)}, bf16[96,1024]{1,0:T(8,128)(2,1)S(1)}, u32[]{:S(2)}, u32[]{:S(2)}) collective-permute-start(bf16[96,1024]{1,0:T(8,128)(2,1)S(1)} %get-tuple-element.75.refs_4_.refs_1_), channel_id=1, source_target_pairs={{0,16},{8,24},{16,0},{24,8},{32,48},{40,56},{48,32},{56,40},{64,80... | collective-permute-start | bytes 589832 | tf_op jit(solution)/shard_map/ppermute | solution.py:53
  68.5 0.0 collective-permute-done.11.refs_3_
  68.5 2.3 %shard_map.129 = (bf16[512,4096]{1,0:T(8,128)(2,1)}, f32[512,512]{1,0:T(8,128)S(1)}) custom-call(bf16[512,512]{1,0:T(8,128)(2,1)S(1)} %get-tuple-element.47.refs_0_.refs_1_, bf16[512,4096]{1,0:T(8,128)(2,1)S(1)} %bitcast.8, bf16[256,1536]{1,0:T(8,128)(2,1)S(1)} %get-tuple-element.70.refs_8_.refs_2_, bf16[256,1536]{1,0:T(8,128)(2,1)S(1)} %collective-permute-done.11.refs_3_, ...), custom_call_target="tpu_custom_call" | custom-call | flops 1 | bytes 1024 | tf_op jit(solution)/shard_map/pallas_call | solution.py:32
  70.8 0.0 collective-permute-done.9.refs_1_.refs_3_
  70.8 0.0 collective-permute-done.10.refs_2_.refs_4_
  70.9 0.2 shard_map.130
  71.0 0.7 collective-permute-start.14
  71.8 0.0 collective-permute-start.15
  71.8 2.7 %collective-permute-start.16 = (bf16[64,1664]{1,0:T(8,128)(2,1)S(1)}, bf16[64,1664]{1,0:T(8,128)(2,1)S(1)}, u32[]{:S(2)}, u32[]{:S(2)}) collective-permute-start(bf16[64,1664]{1,0:T(8,128)(2,1)S(1)} %get-tuple-element.80), channel_id=1, source_target_pairs={{0,3},{1,0},{2,1},{3,2},{4,7},{5,4},{6,5},{7,6},{8,11},{9,8},{10,9... | collective-permute-start | bytes 638984 | tf_op jit(solution)/shard_map/ppermute | solution.py:44
  74.4 4.0 %collective-permute-start.17 = (bf16[96,1024]{1,0:T(8,128)(2,1)S(1)}, bf16[96,1024]{1,0:T(8,128)(2,1)S(1)}, u32[]{:S(2)}, u32[]{:S(2)}) collective-permute-start(bf16[96,1024]{1,0:T(8,128)(2,1)S(1)} %get-tuple-element.75.refs_4_.refs_1_), channel_id=1, source_target_pairs={{0,8},{8,0},{16,24},{24,16},{32,40},{40,32},{48,56},{56,48},{64,72... | collective-permute-start | bytes 589832 | tf_op jit(solution)/shard_map/ppermute | solution.py:53
  78.4 0.0 collective-permute-done.18.refs_0_
  78.4 0.1 collective-permute-start.19
  78.5 0.0 copy-start.4
  78.5 3.2 %shard_map.131 = (bf16[512,4096]{1,0:T(8,128)(2,1)}, bf16[512,512]{1,0:T(8,128)(2,1)}, f32[8,128]{1,0:T(8,128)S(1)}) custom-call(bf16[512,4096]{1,0:T(8,128)(2,1)} %get-tuple-element.81.refs_0_, bf16[512,512]{1,0:T(8,128)(2,1)S(1)} %get-tuple-element.47.refs_0_.refs_1_, bf16[512,4096]{1,0:T(8,128)(2,1)S(1)} %bitcast.9, ...), custom_call_target="tpu_custom_call", output_to_operand_aliasing={{0}: (0, {})} | custom-call | flops 1 | bytes 1024 | tf_op jit(solution)/shard_map/pallas_call | solution.py:32
  81.8 0.0 collective-permute-done.17.refs_2_
  81.8 0.0 collective-permute-done.19.refs_4_
  81.8 1.3 %shard_map.134 = bf16[96,4096]{1,0:T(8,128)(2,1)} custom-call(bf16[96,4096]{1,0:T(8,128)(2,1)S(1)} %bitcast.11, bf16[96,1024]{1,0:T(8,128)(2,1)S(1)} %get-tuple-element.75.refs_4_.refs_1_, bf16[96,1024]{1,0:T(8,128)(2,1)S(1)} %collective-permute-done.17.refs_2_, bf16[96,1024]{1,0:T(8,128)(2,1)S(1)} %shard_map.133.refs_3_, ...), custom_call_target="tpu_custom_call" | custom-call | flops 1 | bytes 1024 | tf_op jit(solution)/shard_map/pallas_call | solution.py:32
  83.1 0.0 collective-permute-done.15.refs_5_
  83.1 0.0 collective-permute-done.16.refs_6_
  83.1 0.0 collective-permute-done.14.refs_3_
  83.1 1.0 %shard_map.132 = bf16[64,4096]{1,0:T(8,128)(2,1)} custom-call(bf16[64,2560]{1,0:T(8,128)(2,1)S(1)} %get-tuple-element.57.refs_0_, bf16[64,8448]{1,0:T(8,128)(2,1)S(1)} %collective-permute-done.9.refs_1_.refs_3_, bf16[64,8448]{1,0:T(8,128)(2,1)S(1)} %collective-permute-done.10.refs_2_.refs_4_, bf16[64,2560]{1,0:T(8,128)(2,1)S(1)} %collective-permute-done.14.refs_3_, ...), custom_call_target="tpu_custom_call" | custom-call | flops 1 | bytes 1024 | tf_op jit(solution)/shard_map/pallas_call | solution.py:32
  (10 shorter events, 0.1 us)
Async XLA Ops:
  0.6 5.0 %copy-start.2 = (bf16[64,4096]{1,0:T(8,128)(2,1)S(1)}, bf16[64,4096]{1,0:T(8,128)(2,1)}, u32[]{:S(2)}) copy-start(bf16[64,4096]{1,0:T(8,128)(2,1)} %refs_2_.3) | copy-start | bytes 1572868
  0.6 1.5 %copy-start.3 = (f32[1,96,4096]{2,1,0:T(8,128)S(1)}, f32[1,96,4096]{2,1,0:T(8,128)}, u32[]{:S(2)}) copy-start(f32[1,96,4096]{2,1,0:T(8,128)} %param.10) | copy-start | bytes 4718596
  2.1 7.4 %copy-start.5 = (bf16[512,512]{1,0:T(8,128)(2,1)S(1)}, bf16[512,512]{1,0:T(8,128)(2,1)}, u32[]{:S(2)}) copy-start(bf16[512,512]{1,0:T(8,128)(2,1)} %refs_0_.1) | copy-start | bytes 1572868
  2.3 10.3 %collective-permute-start = (bf16[96,2048]{1,0:T(8,128)(2,1)S(1)}, bf16[96,2048]{1,0:T(8,128)(2,1)S(1)}, u32[]{:S(2)}, u32[]{:S(2)}) collective-permute-start(bf16[96,2048]{1,0:T(8,128)(2,1)S(1)} %get-tuple-element.49), channel_id=1, source_target_pairs={{0,8},{8,0},{16,24},{24,16},{32,40},{40,32},{48,56},{56,48},{64,72... | collective-permute-start | bytes 1179656 | tf_op jit(solution)/shard_map/ppermute | solution.py:53
  5.7 14.7 %collective-permute-start.3 = (bf16[64,4096]{1,0:T(8,128)(2,1)S(1)}, bf16[64,4096]{1,0:T(8,128)(2,1)S(1)}, u32[]{:S(2)}, u32[]{:S(2)}) collective-permute-start(bf16[64,4096]{1,0:T(8,128)(2,1)S(1)} %copy-done.2), channel_id=1, source_target_pairs={{0,1},{1,2},{2,3},{3,0},{4,5},{5,6},{6,7},{7,4},{8,9},{9,10},{10,1... | collective-permute-start | bytes 1572872 | tf_op jit(solution)/shard_map/ppermute | solution.py:44
  5.7 14.7 %collective-permute-start.4 = (bf16[64,4096]{1,0:T(8,128)(2,1)S(1)}, bf16[64,4096]{1,0:T(8,128)(2,1)S(1)}, u32[]{:S(2)}, u32[]{:S(2)}) collective-permute-start(bf16[64,4096]{1,0:T(8,128)(2,1)S(1)} %copy-done.2), channel_id=1, source_target_pairs={{0,3},{1,0},{2,1},{3,2},{4,7},{5,4},{6,5},{7,6},{8,11},{9,8},{10,9... | collective-permute-start | bytes 1572872 | tf_op jit(solution)/shard_map/ppermute | solution.py:44
  8.4 10.2 %collective-permute-start.2 = (bf16[64,2560]{1,0:T(8,128)(2,1)S(1)}, bf16[64,2560]{1,0:T(8,128)(2,1)S(1)}, u32[]{:S(2)}, u32[]{:S(2)}) collective-permute-start(bf16[64,2560]{1,0:T(8,128)(2,1)S(1)} %slice.3), channel_id=1, source_target_pairs={{0,4},{1,5},{2,6},{3,7},{4,0},{5,1},{6,2},{7,3},{8,12},{9,13},{10,... | collective-permute-start | bytes 983048 | tf_op jit(solution)/shard_map/ppermute | solution.py:49
  9.5 2.2 %copy-start = (bf16[1,512,4096]{2,1,0:T(8,128)(2,1)S(1)}, bf16[1,512,4096]{2,1,0:T(8,128)(2,1)}, u32[]{:S(2)}) copy-start(bf16[1,512,4096]{2,1,0:T(8,128)(2,1)} %param.8) | copy-start | bytes 12582916
  12.9 13.0 %copy-start.6 = (f32[96,128]{1,0:T(8,128)S(1)}, f32[96,128]{1,0:T(8,128)}, u32[]{:S(2)}) copy-start(f32[96,128]{1,0:T(8,128)} %refs_3_.3) | copy-start | bytes 147460
  12.9 13.0 %copy-start.7 = (f32[96,128]{1,0:T(8,128)S(1)}, f32[96,128]{1,0:T(8,128)}, u32[]{:S(2)}) copy-start(f32[96,128]{1,0:T(8,128)} %refs_4_.1) | copy-start | bytes 147460
  12.9 8.3 %collective-permute-start.1 = (bf16[96,1024]{1,0:T(8,128)(2,1)S(1)}, bf16[96,1024]{1,0:T(8,128)(2,1)S(1)}, u32[]{:S(2)}, u32[]{:S(2)}) collective-permute-start(bf16[96,1024]{1,0:T(8,128)(2,1)S(1)} %get-tuple-element.52), channel_id=1, source_target_pairs={{0,16},{8,24},{16,0},{24,8},{32,48},{40,56},{48,32},{56,40},{64,80... | collective-permute-start | bytes 589832 | tf_op jit(solution)/shard_map/ppermute | solution.py:53
  21.2 11.7 %copy-start.1 = (bf16[1,512,4096]{2,1,0:T(8,128)(2,1)S(1)}, bf16[1,512,4096]{2,1,0:T(8,128)(2,1)}, u32[]{:S(2)}) copy-start(bf16[1,512,4096]{2,1,0:T(8,128)(2,1)} %param.8) | copy-start | bytes 12582916
  21.4 19.6 %collective-permute-start.7 = (bf16[256,1536]{1,0:T(8,128)(2,1)S(1)}, bf16[256,1536]{1,0:T(8,128)(2,1)S(1)}, u32[]{:S(2)}, u32[]{:S(2)}) collective-permute-start(bf16[256,1536]{1,0:T(8,128)(2,1)S(1)} %get-tuple-element.62), channel_id=1, source_target_pairs={{0,4},{1,5},{2,6},{3,7},{4,0},{5,1},{6,2},{7,3},{8,12},{9,13},{10,... | collective-permute-start | bytes 2359304 | tf_op jit(solution)/shard_map/ppermute | solution.py:49
  23.2 17.8 %collective-permute-start.5 = (bf16[64,5888]{1,0:T(8,128)(2,1)S(1)}, bf16[64,5888]{1,0:T(8,128)(2,1)S(1)}, u32[]{:S(2)}, u32[]{:S(2)}) collective-permute-start(bf16[64,5888]{1,0:T(8,128)(2,1)S(1)} %get-tuple-element.55.refs_4_), channel_id=1, source_target_pairs={{0,1},{1,2},{2,3},{3,0},{4,5},{5,6},{6,7},{7,4},{8,9},{9,10},{10,1... | collective-permute-start | bytes 2261000 | tf_op jit(solution)/shard_map/ppermute | solution.py:44
  23.2 17.8 %collective-permute-start.6 = (bf16[64,5888]{1,0:T(8,128)(2,1)S(1)}, bf16[64,5888]{1,0:T(8,128)(2,1)S(1)}, u32[]{:S(2)}, u32[]{:S(2)}) collective-permute-start(bf16[64,5888]{1,0:T(8,128)(2,1)S(1)} %get-tuple-element.60), channel_id=1, source_target_pairs={{0,3},{1,0},{2,1},{3,2},{4,7},{5,4},{6,5},{7,6},{8,11},{9,8},{10,9... | collective-permute-start | bytes 2261000 | tf_op jit(solution)/shard_map/ppermute | solution.py:44
  26.0 10.4 %collective-permute-start.8 = (bf16[96,1152]{1,0:T(8,128)(2,1)S(1)}, bf16[96,1152]{1,0:T(8,128)(2,1)S(1)}, u32[]{:S(2)}, u32[]{:S(2)}) collective-permute-start(bf16[96,1152]{1,0:T(8,128)(2,1)S(1)} %get-tuple-element.56.refs_2_.refs_1_), channel_id=1, source_target_pairs={{0,128},{8,136},{16,144},{24,152},{32,160},{40,168},{48,176},{56,1... | collective-permute-start | bytes 663560 | tf_op jit(solution)/shard_map/ppermute | solution.py:53
  41.4 29.4 %collective-permute-start.9 = (bf16[64,8448]{1,0:T(8,128)(2,1)S(1)}, bf16[64,8448]{1,0:T(8,128)(2,1)S(1)}, u32[]{:S(2)}, u32[]{:S(2)}) collective-permute-start(bf16[64,8448]{1,0:T(8,128)(2,1)S(1)} %get-tuple-element.65), channel_id=1, source_target_pairs={{0,1},{1,2},{2,3},{3,0},{4,5},{5,6},{6,7},{7,4},{8,9},{9,10},{10,1... | collective-permute-start | bytes 3244040 | tf_op jit(solution)/shard_map/ppermute | solution.py:44
  41.5 29.4 %collective-permute-start.10 = (bf16[64,8448]{1,0:T(8,128)(2,1)S(1)}, bf16[64,8448]{1,0:T(8,128)(2,1)S(1)}, u32[]{:S(2)}, u32[]{:S(2)}) collective-permute-start(bf16[64,8448]{1,0:T(8,128)(2,1)S(1)} %get-tuple-element.66), channel_id=1, source_target_pairs={{0,3},{1,0},{2,1},{3,2},{4,7},{5,4},{6,5},{7,6},{8,11},{9,8},{10,9... | collective-permute-start | bytes 3244040 | tf_op jit(solution)/shard_map/ppermute | solution.py:44
  44.2 24.4 %collective-permute-start.11 = (bf16[256,1536]{1,0:T(8,128)(2,1)S(1)}, bf16[256,1536]{1,0:T(8,128)(2,1)S(1)}, u32[]{:S(2)}, u32[]{:S(2)}) collective-permute-start(bf16[256,1536]{1,0:T(8,128)(2,1)S(1)} %get-tuple-element.70.refs_8_.refs_2_), channel_id=1, source_target_pairs={{0,4},{1,5},{2,6},{3,7},{4,0},{5,1},{6,2},{7,3},{8,12},{9,13},{10,... | collective-permute-start | bytes 2359304 | tf_op jit(solution)/shard_map/ppermute | solution.py:49
  45.4 14.0 %collective-permute-start.12 = (bf16[96,1280]{1,0:T(8,128)(2,1)S(1)}, bf16[96,1280]{1,0:T(8,128)(2,1)S(1)}, u32[]{:S(2)}, u32[]{:S(2)}) collective-permute-start(bf16[96,1280]{1,0:T(8,128)(2,1)S(1)} %get-tuple-element.64.refs_9_.refs_1_), channel_id=1, source_target_pairs={{0,64},{8,72},{16,80},{24,88},{32,96},{40,104},{48,112},{56,120},{... | collective-permute-start | bytes 737288 | tf_op jit(solution)/shard_map/ppermute | solution.py:53
  59.5 7.1 %collective-permute-start.13 = (bf16[96,1536]{1,0:T(8,128)(2,1)S(1)}, bf16[96,1536]{1,0:T(8,128)(2,1)S(1)}, u32[]{:S(2)}, u32[]{:S(2)}) collective-permute-start(bf16[96,1536]{1,0:T(8,128)(2,1)S(1)} %get-tuple-element.74.refs_1_), channel_id=1, source_target_pairs={{0,32},{8,40},{16,48},{24,56},{32,0},{40,8},{48,16},{56,24},{64,96... | collective-permute-start | bytes 884744 | tf_op jit(solution)/shard_map/ppermute | solution.py:53
  67.3 11.1 %collective-permute-start.18 = (bf16[96,1024]{1,0:T(8,128)(2,1)S(1)}, bf16[96,1024]{1,0:T(8,128)(2,1)S(1)}, u32[]{:S(2)}, u32[]{:S(2)}) collective-permute-start(bf16[96,1024]{1,0:T(8,128)(2,1)S(1)} %get-tuple-element.75.refs_4_.refs_1_), channel_id=1, source_target_pairs={{0,16},{8,24},{16,0},{24,8},{32,48},{40,56},{48,32},{56,40},{64,80... | collective-permute-start | bytes 589832 | tf_op jit(solution)/shard_map/ppermute | solution.py:53
  71.0 12.1 %collective-permute-start.14 = (bf16[64,2560]{1,0:T(8,128)(2,1)S(1)}, bf16[64,2560]{1,0:T(8,128)(2,1)S(1)}, u32[]{:S(2)}, u32[]{:S(2)}) collective-permute-start(bf16[64,2560]{1,0:T(8,128)(2,1)S(1)} %get-tuple-element.77), channel_id=1, source_target_pairs={{0,4},{1,5},{2,6},{3,7},{4,0},{5,1},{6,2},{7,3},{8,12},{9,13},{10,... | collective-permute-start | bytes 983048 | tf_op jit(solution)/shard_map/ppermute | solution.py:49
  71.8 11.4 %collective-permute-start.15 = (bf16[64,1664]{1,0:T(8,128)(2,1)S(1)}, bf16[64,1664]{1,0:T(8,128)(2,1)S(1)}, u32[]{:S(2)}, u32[]{:S(2)}) collective-permute-start(bf16[64,1664]{1,0:T(8,128)(2,1)S(1)} %get-tuple-element.79.refs_8_.refs_1_), channel_id=1, source_target_pairs={{0,1},{1,2},{2,3},{3,0},{4,5},{5,6},{6,7},{7,4},{8,9},{9,10},{10,1... | collective-permute-start | bytes 638984 | tf_op jit(solution)/shard_map/ppermute | solution.py:44
  71.8 11.4 %collective-permute-start.16 = (bf16[64,1664]{1,0:T(8,128)(2,1)S(1)}, bf16[64,1664]{1,0:T(8,128)(2,1)S(1)}, u32[]{:S(2)}, u32[]{:S(2)}) collective-permute-start(bf16[64,1664]{1,0:T(8,128)(2,1)S(1)} %get-tuple-element.80), channel_id=1, source_target_pairs={{0,3},{1,0},{2,1},{3,2},{4,7},{5,4},{6,5},{7,6},{8,11},{9,8},{10,9... | collective-permute-start | bytes 638984 | tf_op jit(solution)/shard_map/ppermute | solution.py:44
  74.4 7.3 %collective-permute-start.17 = (bf16[96,1024]{1,0:T(8,128)(2,1)S(1)}, bf16[96,1024]{1,0:T(8,128)(2,1)S(1)}, u32[]{:S(2)}, u32[]{:S(2)}) collective-permute-start(bf16[96,1024]{1,0:T(8,128)(2,1)S(1)} %get-tuple-element.75.refs_4_.refs_1_), channel_id=1, source_target_pairs={{0,8},{8,0},{16,24},{24,16},{32,40},{40,32},{48,56},{56,48},{64,72... | collective-permute-start | bytes 589832 | tf_op jit(solution)/shard_map/ppermute | solution.py:53
  78.4 3.4 %collective-permute-start.19 = (bf16[96,1024]{1,0:T(8,128)(2,1)S(1)}, bf16[96,1024]{1,0:T(8,128)(2,1)S(1)}, u32[]{:S(2)}, u32[]{:S(2)}) collective-permute-start(bf16[96,1024]{1,0:T(8,128)(2,1)S(1)} %shard_map.133.refs_3_), channel_id=1, source_target_pairs={{0,8},{8,0},{16,24},{24,16},{32,40},{40,32},{48,56},{56,48},{64,72... | collective-permute-start | bytes 589832 | tf_op jit(solution)/shard_map/ppermute | solution.py:53
  78.5 3.3 %copy-start.4 = (bf16[1,96,4096]{2,1,0:T(8,128)(2,1)S(1)}, bf16[1,96,4096]{2,1,0:T(8,128)(2,1)}, u32[]{:S(2)}) copy-start(bf16[1,96,4096]{2,1,0:T(8,128)(2,1)} %param.11) | copy-start | bytes 2359300
